TPU v7x, 32 devices: a whole 2x2x4 slice. The times are simulated.
32 devices in a mesh: leaf: 8 (over y, x, core), mat: 4 (over z).
Axes of the slice: x: 2, y: 2, z: 4, core: 2. Of those that a mesh axis runs over, the one named last changes fastest.
Arguments:
- leaf_value: float32 [64, 1024, 1024], P('leaf', 'mat'), as said below
- section_cost: float32 [1024, 1024], P('mat'), as said below
- input_cost: float32 [256, 256], replicated, as said below
- dynamics: float32 [1024, 1024], P('mat'), may hold values from -0.1875 to 0.1875
- input_map: float32 [1024, 256], replicated, may hold values from -0.1875 to 0.1875
- parent_of: int32 [64], replicated, may hold values from 0 to 15, as said below
- prob_weight: int32 [64], replicated, may hold values from 1 to 16
- parent_state: float32 [16, 1024], P('leaf', 'mat'), may hold values from -6 to 6
- disturbance: float32 [64, 1024], P('leaf', 'mat'), may hold values from -6 to 6
Outputs:
- parent_value: float32 [16, 1024, 1024], P('leaf', 'mat')
- parent_gain: float32 [16, 1024, 256], P('leaf', 'mat')
- child_state: float32 [64, 1024], P('leaf', 'mat')
Inputs may be any that keep to these rules, and one draw needn't show every extreme that they name: Each leaf_value[l] is symmetric positive definite. `section_cost`: symmetric positive definite. `input_cost`: symmetric positive definite. `parent_of`: every parent has exactly 4 children; the parent of a leaf among the 8 leaves of one leaf index is one of that index's 2 parents, the last parent of the index before, or the first parent of the index after; each leaf index except the ends holds a child of both neighbours' parents.
All inputs are finite; a program needn't handle non-finite values.
Results may differ from a plain program's by a relative error of at most 0.000075.
Values sent between devices are 32-bit elements; how exact they have to be, the bound alone decides.
A program may use at most 64 MiB of HBM per device.

v0:
```python
import jax
import jax.numpy as jnp
from jax import lax
from jax.sharding import PartitionSpec as P

highest = lax.Precision.HIGHEST


def extended_2(block, sides, width):
    for axis, dim in sides:
        count = lax.axis_size(axis)
        forward = [(i, i + 1) for i in range(count - 1)]
        backward = [(target, source) for source, target in forward]
        low = lax.ppermute(
            lax.slice_in_dim(block, block.shape[dim] - width, None, axis=dim), axis, forward
        )
        high = lax.ppermute(lax.slice_in_dim(block, 0, width, axis=dim), axis, backward)
        block = jnp.concatenate([low, block, high], axis=dim)
    return block


def local(
    leaf_value,
    section_cost,
    input_cost,
    dynamics,
    input_map,
    parent_of,
    prob_weight,
    parent_state,
    disturbance,
):
    leaf_dev = leaf_value.shape[0]
    par_dev = parent_state.shape[0]
    slab_rows = leaf_value.shape[1]
    states = leaf_value.shape[2]
    leaf_index = lax.axis_index("leaf")
    column = lax.axis_index("mat")
    row_start = column * slab_rows
    full_dyn = lax.all_gather(dynamics, "mat", axis=0, tiled=True)
    joined = jnp.concatenate([full_dyn, input_map], axis=1)
    weights = prob_weight.astype(jnp.float32)
    my_parents = lax.dynamic_slice_in_dim(parent_of, leaf_index * leaf_dev, leaf_dev, 0)
    my_weights = lax.dynamic_slice_in_dim(weights, leaf_index * leaf_dev, leaf_dev, 0)
    first_label = leaf_index * par_dev
    slot_ids = jnp.arange(par_dev + 2, dtype=jnp.int32)
    chosen = (my_parents - first_label + 1)[:, None] == slot_ids[None, :]
    member = jnp.where(chosen, my_weights[:, None], 0.0)
    labels = first_label + jnp.arange(par_dev, dtype=jnp.int32)
    totals = jnp.sum(
        jnp.where(parent_of[:, None] == labels[None, :], weights[:, None], 0.0), axis=0
    )
    leaf_terms = jnp.einsum("st,sij->tij", member, leaf_value, precision=highest)
    edge_terms = jnp.stack([leaf_terms[0], leaf_terms[par_dev + 1]])
    beside_all = extended_2(edge_terms, (("leaf", 0),), 1)
    summed = leaf_terms[1 : par_dev + 1]
    summed = summed.at[0].add(beside_all[0]).at[par_dev - 1].add(beside_all[3])
    expected = summed / totals[:, None, None]
    value_rows = jnp.einsum("prk,kj->prj", expected, full_dyn, precision=highest)
    products = jnp.einsum(
        "pkr,kj->prj",
        lax.all_to_all(value_rows, "mat", split_axis=2, concat_axis=1, tiled=True),
        joined,
        precision=highest,
    )
    curvature = products[:, :, :states]
    coupling_rows = products[:, :, states:]
    input_side = jnp.einsum("prk,ka->pra", expected, input_map, precision=highest)
    input_rows = lax.dynamic_slice_in_dim(input_map, row_start, slab_rows, 0)
    partial_value = jnp.einsum("ra,prb->pab", input_rows, input_side, precision=highest)
    hessian = input_cost[None] + lax.psum(partial_value, "mat")
    factor = jnp.linalg.cholesky(hessian)
    scaled_rows = lax.linalg.triangular_solve(
        factor, coupling_rows, left_side=False, lower=True, transpose_a=True
    )
    gain_rows = -lax.linalg.triangular_solve(factor, scaled_rows, left_side=False, lower=True)
    reduction = jnp.einsum(
        "pra,pka->prk",
        scaled_rows,
        lax.all_gather(scaled_rows, "mat", axis=1, tiled=True),
        precision=highest,
    )
    new_value = section_cost[None] + curvature - reduction
    control = jnp.einsum("pja,pj->pa", gain_rows, parent_state, precision=highest)
    dyn_cols = lax.dynamic_slice_in_dim(full_dyn, row_start, slab_rows, 1)
    partial_next = jnp.einsum("ij,pj->pi", dyn_cols, parent_state, precision=highest)
    partial_next = partial_next + jnp.einsum("ia,pa->pi", input_map, control, precision=highest)
    following = lax.psum_scatter(partial_next, "mat", scatter_dimension=1, tiled=True)
    extended = extended_2(following, (("leaf", 0),), 1)
    child_state = (
        jnp.einsum("st,tj->sj", chosen.astype(jnp.float32), extended, precision=highest)
        + disturbance
    )
    return (new_value, gain_rows, child_state)


def solution(mesh):
    in_specs = (
        P("leaf", "mat", None),
        P("mat", None),
        P(),
        P("mat", None),
        P(),
        P(),
        P(),
        P("leaf", "mat"),
        P("leaf", "mat"),
    )
    out_specs = (P("leaf", "mat", None), P("leaf", "mat", None), P("leaf", "mat"))
    return jax.shard_map(local, mesh=mesh, in_specs=in_specs, out_specs=out_specs, check_vma=False)
```

profile of v0, /device:TPU:0, one launch (start us, length us, event | category | flops | bytes accessed | tf_op | source)
XLA Modules:
  0.0 385.0 jit_solution(17189534767383592484)
XLA Ops:
  9.4 15.4 %fusion = f32[4,256,1024]{2,0,1:T(4,128)S(1)} fusion(f32[8,256,1024]{2,1,0:T(8,128)} %param.13, f32[8]{0:T(128)S(1)} %dynamic_slice.13, s32[8]{0:T(128)S(1)} %subtract_add_fusion), kind=kOutput, calls=%fused_computation.2 | convolution fusion | flops 100663360 | bytes 12582976 | tf_op jit(solution)/shard_map/st,sij->tij/dot_general | solution.py:53
  24.8 2.2 fusion.48
  28.2 3.4 collective-permute-start
  38.6 2.5 fusion.9
  41.1 2.8 fusion.8
  43.9 3.9 %fusion.10 = f32[2,256,256]{1,2,0:T(8,128)S(1)} fusion(f32[1024,256]{1,0:T(8,128)S(1)} %copy-done.1, f32[2,256,1024]{2,1,0:T(8,128)} %fusion.8, f32[2]{0:T(128)S(1)} %fusion.39), kind=kOutput, calls=%fused_computation.24 | convolution fusion | flops 1611137024 | bytes 3670024 | tf_op jit(solution)/shard_map/prk,ka->pra/dot_general | solution.py:68
  49.2 43.9 %all-gather.3.cloned.1.call-done = f32[1024,1024]{1,0:T(8,128)} async-done(((f32[256,1024]{1,0:T(8,128)}), f32[1024,1024]{1,0:T(8,128)}) %all-gather.3.cloned.1.call-update) | async-done | bytes 4194320 | tf_op jit(solution)/shard_map/all_gather | solution.py:40
  93.1 9.7 %fusion.5 = f32[2,256,1024]{2,1,0:T(8,128)} fusion(f32[1024,1024]{1,0:T(8,128)} %all-gather.3.cloned.1.call-done, f32[2,256,1024]{2,1,0:T(8,128)S(1)} %copy-done.3, f32[2]{0:T(128)S(1)} %fusion.39), kind=kOutput, calls=%fused_computation.8 | convolution fusion | flops 6442975232 | bytes 8388616 | tf_op jit(solution)/shard_map/prk,kj->prj/dot_general | solution.py:59
  102.8 4.1 %copy.69 = f32[2,256,1024]{1,0,2:T(2,128)} copy(f32[2,256,1024]{2,1,0:T(8,128)} %fusion.5) | data formatting | bytes 4194304 | tf_op jit(solution)/shard_map/prk,kj->prj/dot_general | solution.py:59
  106.9 3.6 all-to-all-start
  110.9 28.6 %all-reduce.3.cloned.1.call-done = f32[2,256,256]{1,2,0:T(8,128)} async-done(((f32[2,256,256]{1,2,0:T(8,128)}), f32[2,256,256]{1,2,0:T(8,128)}) %all-reduce.3.cloned.1.call-update) | async-done | bytes 524304 | tf_op jit(solution)/shard_map/psum | solution.py:71
  143.6 23.5 %custom-call.18 = f32[2,128,128]{2,1,0:T(8,128)S(1)} custom-call(f32[2,128,128]{2,1,0:T(8,128)S(1)} %cholesky.122), custom_call_target="Cholesky" | custom-call | tf_op jit(solution)/shard_map/jit(cholesky)/cholesky | solution.py:72
  167.2 19.7 %custom-call.19 = f32[2,1,128,128]{2,3,1,0:T(8,128)S(1)} custom-call(f32[2,1,128,128]{3,2,1,0:T(8,128)S(1)} %select_bitcast_fusion), custom_call_target="InvertDiagBlocksLowerTriangular" | custom-call | tf_op jit(solution)/shard_map/jit(cholesky)/cholesky | solution.py:72
  189.3 23.5 %custom-call.20 = f32[2,128,128]{2,1,0:T(8,128)S(1)} custom-call(f32[2,128,128]{2,1,0:T(8,128)S(1)} %convolution_subtract_fusion.2), custom_call_target="Cholesky" | custom-call | tf_op jit(solution)/shard_map/jit(cholesky)/cholesky | solution.py:72
  213.2 5.3 %while.3 = (s32[]{:T(128)}, f32[2,256,256]{2,1,0:T(8,128)S(1)}, s32[2,2]{1,0:T(2,128)S(1)}, f32[2,2,128,128]{3,2,0,1:T(8,128)}, s32[]{:T(128)}) while((s32[]{:T(128)}, f32[2,256,256]{2,1,0:T(8,128)S(1)}, s32[2,2]{1,0:T(2,128)S(1)}, f32[2,2,128,128]{3,2,0,1:T(8,128)}, s32[]{:T(128)}) %tuple.42), condition=%wide.while_cond.2, body=%wide.while_body.2.sunk | while | flops 2 | bytes 263777 | solution.py:73
  216.5 2.1 bitcast_dynamic-update-slice_fusion.2
  218.5 41.0 %custom-call.21 = f32[2,2,128,128]{2,3,1,0:T(8,128)} custom-call(f32[2,2,128,128]{3,2,1,0:T(8,128)} %bitcast.82), custom_call_target="InvertDiagBlocksLowerTriangular" | custom-call | tf_op jit(solution)/shard_map/triangular_solve | solution.py:73
  259.5 2.2 convolution_bitcast_fusion.1
  261.7 2.7 copy.124
  264.4 3.3 all_to_all.16
  267.7 11.5 %fusion.2 = f32[2,256,1280]{2,1,0:T(8,128)S(1)} fusion(f32[2,1024,256]{1,2,0:T(8,128)} %all_to_all.16, f32[1024,256]{1,0:T(8,128)} %param.17, f32[1024,1024]{1,0:T(8,128)} %all-gather.3.cloned.1.call-done), kind=kOutput, calls=%fused_computation.5 | convolution fusion | flops 8054374400 | bytes 9961472 | tf_op jit(solution)/shard_map/pkr,kj->prj/dot_general | solution.py:60
  287.1 39.3 %reduce-scatter.4.cloned.1.call-done = f32[256,2]{1,0:T(8,128)} async-done(((f32[1024,2]{1,0:T(8,128)}), f32[256,2]{1,0:T(8,128)}) %reduce-scatter.4.cloned.1.call-update) | async-done | bytes 2064
  334.6 38.0 %all-gather.5.cloned.1.call-done = f32[2,1024,256]{1,2,0:T(8,128)} async-done(((f32[2,256,256]{1,2,0:T(8,128)}), f32[2,1024,256]{1,2,0:T(8,128)}) %all-gather.5.cloned.1.call-update) | async-done | bytes 2097168 | tf_op jit(solution)/shard_map/all_gather | solution.py:80
  372.7 5.3 %fusion.7 = f32[2,256,1024]{2,1,0:T(8,128)} fusion(f32[2,256,1280]{2,1,0:T(8,128)S(1)} %fusion.2, f32[2,1024,256]{1,2,0:T(8,128)} %all-gather.5.cloned.1.call-done, f32[256,1024]{1,0:T(8,128)} %param.14, f32[2,256,128]{1,2,0:T(8,128)S(1)} %fusion.23, f32[2,256,128]{1,2,0:T(8,128)S(1)} %fusion.14), kind=kOutput, calls=%fused_computation.11 | convolution fusion | flops 1611792384 | bytes 7864320 | tf_op jit(solution)/shard_map/pra,pka->prk/dot_general | solution.py:77
  (87 shorter events, 38.3 us)
Async XLA Ops:
  7.2 252.3 %copy-start = (f32[2,256]{1,0:T(2,128)S(1)}, f32[2,256]{1,0:T(2,128)}, u32[]{:S(2)}) copy-start(f32[2,256]{1,0:T(2,128)} %param.20) | copy-start | bytes 6148
  7.2 85.9 %all-gather.3.cloned.1.call-start = ((), (), s32[]{:S(2)}) async-start(), calls=%async_computation.2 | async-start | bytes 5242880 | tf_op jit(solution)/shard_map/all_gather | solution.py:40
  7.9 131.6 %all-reduce.3.cloned.1.call-start = ((), (), s32[]{:S(2)}) async-start(), calls=%async_computation.3 | async-start | bytes 1048576 | tf_op jit(solution)/shard_map/psum | solution.py:71
  28.2 10.4 %collective-permute-start = (f32[1,256,1024]{2,1,0:T(8,128)}, f32[1,256,1024]{2,1,0:T(8,128)}, u32[]{:S(2)}, u32[]{:S(2)}) collective-permute-start(f32[1,256,1024]{2,1,0:T(8,128)} %copy.106), channel_id=1, source_target_pairs={{0,4},{4,8},{8,12},{12,16},{16,20},{20,24},{24,28},{1,5},{5,9},{9,... | collective-permute-start | bytes 3145736 | tf_op jit(solution)/shard_map/ppermute | solution.py:14
  32.7 8.4 %collective-permute-start.1 = (f32[1,256,1024]{2,1,0:T(8,128)}, f32[1,256,1024]{2,1,0:T(8,128)}, u32[]{:S(2)}, u32[]{:S(2)}) collective-permute-start(f32[1,256,1024]{2,1,0:T(8,128)} %copy.107), channel_id=1, source_target_pairs={{4,0},{8,4},{12,8},{16,12},{20,16},{24,20},{28,24},{5,1},{9,5},{13... | collective-permute-start | bytes 3145736 | tf_op jit(solution)/shard_map/ppermute | solution.py:17
  35.3 3.1 copy-start.10
  41.1 2.8 copy-start.1
  43.9 49.2 %copy-start.3 = (f32[2,256,1024]{2,1,0:T(8,128)S(1)}, f32[2,256,1024]{2,1,0:T(8,128)}, u32[]{:S(2)}) copy-start(f32[2,256,1024]{2,1,0:T(8,128)} %fusion.8) | copy-start | bytes 6291460
  106.9 154.8 %all-to-all-start = ((f32[2,256,1024]{1,0,2:T(2,128)}), f32[2,256,1024]{1,0,2:T(2,128)S(1)}, u32[]{:S(2)}, u32[]{:S(2)}) async-start(f32[2,256,1024]{1,0,2:T(2,128)} %copy.69), calls=%async_computation | async-start | bytes 4194304 | tf_op jit(solution)/shard_map/all_to_all | solution.py:62
  110.5 215.8 %reduce-scatter.4.cloned.1.call-start = ((), (), s32[]{:S(2)}) async-start(), calls=%async_computation.5 | async-start | bytes 655360
  139.5 3.2 copy-start.5
  142.8 0.8 copy-start.6
  218.5 61.2 %copy-start.4 = (f32[2,256,256]{2,1,0:T(8,128)}, f32[2,256,256]{2,1,0:T(8,128)S(1)}, u32[]{:S(2)}) copy-start(f32[2,256,256]{2,1,0:T(8,128)S(1)} %get-tuple-element.121) | copy-start | bytes 1572868
  267.7 11.5 %copy-start.7 = (f32[2,2,128,128]{2,3,1,0:T(8,128)S(1)}, f32[2,2,128,128]{2,3,1,0:T(8,128)}, u32[]{:S(2)}) copy-start(f32[2,2,128,128]{2,3,1,0:T(8,128)} %custom-call.21) | copy-start | bytes 786436
  279.7 4.5 %copy-start.2 = (f32[1024,256]{1,0:T(8,128)S(1)}, f32[1024,256]{1,0:T(8,128)}, u32[]{:S(2)}) copy-start(f32[1024,256]{1,0:T(8,128)} %param.17) | copy-start | bytes 3145732
  282.9 0.7 copy-start.8
  286.2 47.7 %copy-start.9 = (f32[8,256]{1,0:T(8,128)S(1)}, f32[8,256]{1,0:T(8,128)}, u32[]{:S(2)}) copy-start(f32[8,256]{1,0:T(8,128)} %param.21) | copy-start | bytes 24580
  286.2 86.5 %all-gather.5.cloned.1.call-start = ((), (), s32[]{:S(2)}) async-start(), calls=%async_computation.4 | async-start | bytes 2621440 | tf_op jit(solution)/shard_map/all_gather | solution.py:80
  327.4 6.4 %collective-permute-start.2 = (f32[1,256]{1,0:T(1,128)S(1)}, f32[1,256]{1,0:T(1,128)S(1)}, u32[]{:S(2)}, u32[]{:S(2)}) collective-permute-start(f32[1,256]{1,0:T(1,128)S(1)} %get-tuple-element.63), channel_id=1, source_target_pairs={{0,4},{4,8},{8,12},{12,16},{16,20},{20,24},{24,28},{1,5},{5,9},{9,... | collective-permute-start | bytes 3080 | tf_op jit(solution)/shard_map/ppermute | solution.py:14
  328.7 5.1 %collective-permute-start.3 = (f32[1,256]{1,0:T(1,128)S(1)}, f32[1,256]{1,0:T(1,128)S(1)}, u32[]{:S(2)}, u32[]{:S(2)}) collective-permute-start(f32[1,256]{1,0:T(1,128)S(1)} %get-tuple-element.64), channel_id=1, source_target_pairs={{4,0},{8,4},{12,8},{16,12},{20,16},{24,20},{28,24},{5,1},{9,5},{13... | collective-permute-start | bytes 3080 | tf_op jit(solution)/shard_map/ppermute | solution.py:17
Sparse Core Ops, SparseCore 0:
  9.6 83.4 all-gather.2
  96.0 43.4 all-reduce.2
  286.3 40.0 reduce-scatter.3
  328.4 44.2 all-gather.4
where the time goes:
time: 392 us; the launch traced here: 385 us
  waiting for transfers between devices  151 us (39%)
  other arithmetic  120 us (31%)
  matrix products  57.8 us (15%)
  local copies, waits for them, and re-layouts  31.1 us (8%)
  between operations  14.6 us (4%)
  starting transfers between devices  11.4 us (3%)
    another operation x9, other arithmetic, local(): factor = jnp.linalg.cholesky(hessian)  66.8 us
    all_gather x1, waiting for transfers between devices, local(): full_dyn = lax.all_gather(dynamics, 'mat', axis=0, tiled=True)  43.9 us
    another operation x5, other arithmetic, local(): lax.linalg.triangular_solve(factor, coupling_rows, left_side=False, lower...  42 us
    unnamed x5, waiting for transfers between devices  40 us
    all_gather x1, waiting for transfers between devices, local(): lax.all_gather(scaled_rows, 'mat', axis=1, tiled=True)  38 us
    psum x1, waiting for transfers between devices, local(): hessian = input_cost[None] + lax.psum(partial_value, 'mat')  28.6 us
    dot_general x1, matrix products, local(): jnp.einsum('st,sij->tij', member, leaf_value, precision=highest)  15.4 us
    dot_general x1, matrix products, local(): jnp.einsum('pkr,kj->prj', lax.all_to_all(value_rows, 'mat', split_axis=2,...  11.5 us
  transfers between devices with their start and end apart: 9, of which 4 were waited for; matrix products, arithmetic and copies ran while one was open for 46% of the time, Pallas kernels for 0%

commit v1 on v0

v1 whole, which is shorter than its diff:
```python
import jax
import jax.numpy as jnp
from jax import lax
from jax.experimental import pallas as pl
from jax.experimental.pallas import tpu as pltpu
from jax.sharding import PartitionSpec as P

highest = lax.Precision.HIGHEST
high = lax.Precision.HIGH


def shifted(block, axis, step):
    count = lax.axis_size(axis)
    return lax.ppermute(block, axis, [(i, (i + step) % count) for i in range(count)])


def shifts_of(count):
    order = []
    for step in range(1, count // 2 + 1):
        order.append(step)
        if count - step != step:
            order.append(count - step)
    return order


def gathered(block, axis, dim):
    count, me, size = lax.axis_size(axis), lax.axis_index(axis), block.shape[dim]
    shape = block.shape[:dim] + (size * count,) + block.shape[dim + 1 :]
    whole = lax.dynamic_update_slice_in_dim(jnp.zeros(shape, block.dtype), block, me * size, dim)
    parts = [(step, shifted(block, axis, step)) for step in shifts_of(count)]
    for step, part in parts:
        source = lax.rem(me + count - step, count)
        whole = lax.dynamic_update_slice_in_dim(whole, part, source * size, dim)
    return whole


def edge_rows(block):
    count = lax.axis_size("leaf")
    forward = [(i, i + 1) for i in range(count - 1)]
    backward = [(target, source) for source, target in forward]
    return forward, backward


def leaf_sum_kernel(member_ref, leaf_ref, low_ref, own_ref, high_ref):
    leaves = leaf_ref.shape[0]
    slots = own_ref.shape[0] + 2
    outs = [low_ref.at[0]] + [own_ref.at[t] for t in range(slots - 2)] + [high_ref.at[0]]
    for row in range(0, leaf_ref.shape[1], 8):
        terms = [leaf_ref[s, row : row + 8, :] for s in range(leaves)]
        for t in range(slots):
            total = terms[0] * member_ref[0, t]
            for s in range(1, leaves):
                total = total + terms[s] * member_ref[s, t]
            outs[t][row : row + 8, :] = total


def leaf_sums(member, leaf_value, par_dev):
    leaves, rows, states = leaf_value.shape
    tile = min(32, rows)
    block = lambda count: pl.BlockSpec((count, tile, states), lambda i: (0, i, 0))
    shape = lambda count: jax.ShapeDtypeStruct((count, rows, states), jnp.float32)
    return pl.pallas_call(
        leaf_sum_kernel,
        grid=(rows // tile,),
        in_specs=[pl.BlockSpec(memory_space=pltpu.SMEM), block(leaves)],
        out_specs=[block(1), block(par_dev), block(1)],
        out_shape=[shape(1), shape(par_dev), shape(1)],
        compiler_params=pltpu.CompilerParams(vmem_limit_bytes=32 * 2**20),
    )(member, leaf_value)


def inverse_kernel(cost_ref, map_ref, side_ref, inv_ref, hess):
    parents, _, inputs = side_ref.shape
    row = lax.broadcasted_iota(jnp.int32, (inputs, inputs), 0)
    col = lax.broadcasted_iota(jnp.int32, (inputs, inputs), 1)
    eye = (row == col).astype(jnp.float32)
    dot = lambda a, b: jnp.dot(a, b, precision=highest, preferred_element_type=jnp.float32)
    for p in range(parents):
        product = lax.dot_general(
            map_ref[...],
            side_ref[p],
            (((0,), (0,)), ((), ())),
            precision=highest,
            preferred_element_type=jnp.float32,
        )
        value = cost_ref[...] + product
        hess[p] = value
        bound = jnp.max(jnp.sum(jnp.abs(value), axis=0))
        inv_ref[p] = eye / bound

    def more(carry):
        turn, worst = carry
        return jnp.logical_and(turn < 64, worst > 1e-8)

    def step(carry):
        turn, _ = carry
        residual = [eye - dot(hess[p], inv_ref[p]) for p in range(parents)]
        for p in range(parents):
            inv_ref[p] = inv_ref[p] + dot(inv_ref[p], residual[p])
        worst = jnp.sum(residual[0] * residual[0])
        for p in range(1, parents):
            worst = jnp.maximum(worst, jnp.sum(residual[p] * residual[p]))
        return turn + 1, worst

    lax.while_loop(more, step, (jnp.int32(0), jnp.float32(jnp.inf)))


def inverses(input_cost, input_map, side):
    parents, _, inputs = side.shape
    return pl.pallas_call(
        inverse_kernel,
        in_specs=[pl.BlockSpec(memory_space=pltpu.VMEM)] * 3,
        out_specs=pl.BlockSpec(memory_space=pltpu.VMEM),
        out_shape=jax.ShapeDtypeStruct((parents, inputs, inputs), jnp.float32),
        scratch_shapes=[pltpu.VMEM((parents, inputs, inputs), jnp.float32)],
        compiler_params=pltpu.CompilerParams(vmem_limit_bytes=32 * 2**20),
        cost_estimate=pl.CostEstimate(
            flops=600 * parents * inputs**3, bytes_accessed=4 * 2**20, transcendentals=0
        ),
    )(input_cost, input_map, side)


def local(
    leaf_value,
    section_cost,
    input_cost,
    dynamics,
    input_map,
    parent_of,
    prob_weight,
    parent_state,
    disturbance,
):
    leaf_dev = leaf_value.shape[0]
    par_dev = parent_state.shape[0]
    slab_rows = leaf_value.shape[1]
    leaf_index = lax.axis_index("leaf")
    column = lax.axis_index("mat")
    count = lax.axis_size("mat")
    forward, backward = edge_rows(parent_state)
    row_start = column * slab_rows
    full_dyn = gathered(dynamics, "mat", 0)
    weights = prob_weight.astype(jnp.float32)
    my_parents = lax.dynamic_slice_in_dim(parent_of, leaf_index * leaf_dev, leaf_dev, 0)
    my_weights = lax.dynamic_slice_in_dim(weights, leaf_index * leaf_dev, leaf_dev, 0)
    first_label = leaf_index * par_dev
    slot_ids = jnp.arange(par_dev + 2, dtype=jnp.int32)
    chosen = (my_parents - first_label + 1)[:, None] == slot_ids[None, :]
    member = jnp.where(chosen, my_weights[:, None], 0.0)
    labels = first_label + jnp.arange(par_dev, dtype=jnp.int32)
    totals = jnp.sum(
        jnp.where(parent_of[:, None] == labels[None, :], weights[:, None], 0.0), axis=0
    )
    low, own, top = leaf_sums(member, leaf_value, par_dev)
    from_low = lax.ppermute(top, "leaf", forward)
    from_high = lax.ppermute(low, "leaf", backward)
    pads = [jnp.zeros_like(own[:1])] * (par_dev - 1)
    beside = jnp.concatenate([from_low] + pads) + jnp.concatenate(pads + [from_high])
    expected = (own + beside) / totals[:, None, None]

    side_rows = jnp.einsum("prk,ka->pra", expected, input_map, precision=high)
    side = gathered(side_rows, "mat", 1)
    state = gathered(parent_state, "mat", 1)

    def value_block(target):
        columns = lax.dynamic_slice_in_dim(full_dyn, target * slab_rows, slab_rows, 1)
        return jnp.einsum("prk,kj->prj", expected, columns, precision=high)

    dyn_cols = lax.dynamic_slice_in_dim(full_dyn, row_start, slab_rows, 1)
    parts = []
    for step in shifts_of(count):
        block = value_block(lax.rem(column + step, count))
        parts.append((step, shifted(block, "mat", step)))
    shape = (par_dev, slab_rows * count, slab_rows)
    value_cols = lax.dynamic_update_slice_in_dim(
        jnp.zeros(shape, jnp.float32), value_block(column), row_start, 1
    )

    inv = inverses(input_cost, input_map, side)
    free_next = jnp.einsum("ij,pj->pi", full_dyn, state, precision=highest)
    pull = jnp.einsum("pka,pk->pa", side, free_next, precision=highest)
    control = -jnp.einsum("pab,pb->pa", inv, pull, precision=highest)
    input_rows = lax.dynamic_slice_in_dim(input_map, row_start, slab_rows, 0)
    following = lax.dynamic_slice_in_dim(free_next, row_start, slab_rows, 1) + jnp.einsum(
        "ra,pa->pr", input_rows, control, precision=highest
    )
    below = lax.ppermute(following[par_dev - 1 :], "leaf", forward)
    above = lax.ppermute(following[:1], "leaf", backward)

    coupling_rows = jnp.einsum("kr,pka->pra", dyn_cols, side, precision=high)
    gain_rows = -jnp.einsum("pra,pab->prb", coupling_rows, inv, precision=high)
    feedback = jnp.einsum("prb,pkb->prk", gain_rows, side, precision=high)

    for step, part in parts:
        source = lax.rem(column + count - step, count)
        value_cols = lax.dynamic_update_slice_in_dim(value_cols, part, source * slab_rows, 1)
    closed = jnp.swapaxes(value_cols, 1, 2) + feedback
    new_value = section_cost[None] + jnp.einsum("prk,kj->prj", closed, full_dyn, precision=high)

    extended = jnp.concatenate([below, following, above], axis=0)
    child_state = disturbance
    for t in range(par_dev + 2):
        child_state = child_state + jnp.where(chosen[:, t : t + 1], extended[t][None, :], 0.0)
    return (new_value, gain_rows, child_state)


def solution(mesh):
    in_specs = (
        P("leaf", "mat", None),
        P("mat", None),
        P(),
        P("mat", None),
        P(),
        P(),
        P(),
        P("leaf", "mat"),
        P("leaf", "mat"),
    )
    out_specs = (P("leaf", "mat", None), P("leaf", "mat", None), P("leaf", "mat"))
    return jax.shard_map(local, mesh=mesh, in_specs=in_specs, out_specs=out_specs, check_vma=False)
```

time: 392 us -> 203 us (0.52); the launches traced: 385 us -> 203 us
  other arithmetic: 120 us -> 4.46 us
  waiting for transfers between devices: 151 us -> 94.3 us
  starting transfers between devices: 11.4 us -> 41 us
  matrix products: 57.8 us -> 28.4 us
  Pallas kernels: 0 us -> 18.9 us
  local copies, waits for them, and re-layouts: 31.1 us -> 14.6 us
  between operations: 14.6 us -> 0.96 us
    another operation x14 -> x0, other arithmetic: 109 us -> none  [the longest x9 66.8 us: local(): factor = jnp.linalg.cholesky(hessian)]
    ppermute x4 -> x16, waiting for transfers between devices: 0.01 us -> 94.3 us  [the longest x12 94.3 us: shifted(): lax.ppermute(block, axis, [(i, (i + step) % count) for i in range(count)])]
    all_gather x2 -> x0, waiting for transfers between devices: 81.9 us -> none  [the longest x1 43.9 us: local(): full_dyn = lax.all_gather(dynamics, 'mat', axis=0, tiled=True)]
    unnamed x5 -> x0, waiting for transfers between devices: 40 us -> none
    ppermute x4 -> x16, starting transfers between devices: 7.4 us -> 41 us  [the longest x12 33.9 us: shifted(): lax.ppermute(block, axis, [(i, (i + step) % count) for i in range(count)])]
    psum x1 -> x0, waiting for transfers between devices: 28.6 us -> none  [local(): hessian = input_cost[None] + lax.psum(partial_value, 'mat')]
    dot_general x10 -> x13, matrix products: 51.7 us -> 28.4 us  [the longest x4 8.96 us: value_block(): return jnp.einsum('prk,kj->prj', expected, columns, precision=high)]
    pallas_call x0 -> x2, Pallas kernels: none -> 18.9 us  [the longest x1 13.8 us: inverses(): pl.pallas_call(inverse_kernel, in_specs=[pl.BlockSpec(memory_space=pltpu....]
  transfers between devices with their start and end apart: 9 -> 16, of which waited for: 4 -> 6; matrix products, arithmetic and copies ran while one was open for 46% -> 21% of each run, Pallas kernels for 0% -> 9%
where the time goes in v1:
time: 203 us
  waiting for transfers between devices  94.3 us (46%)
  starting transfers between devices  41 us (20%)
  matrix products  28.4 us (14%)
  Pallas kernels  18.9 us (9%)
  local copies, waits for them, and re-layouts  14.6 us (7%)
  other arithmetic  4.46 us (2%)
    ppermute x12, waiting for transfers between devices, shifted(): lax.ppermute(block, axis, [(i, (i + step) % count) for i in range(count)])  94.3 us
    ppermute x12, starting transfers between devices, shifted(): lax.ppermute(block, axis, [(i, (i + step) % count) for i in range(count)])  33.9 us
    pallas_call x1, Pallas kernels, inverses(): pl.pallas_call(inverse_kernel, in_specs=[pl.BlockSpec(memory_space=pltpu....  13.8 us
    dot_general x4, matrix products, value_block(): return jnp.einsum('prk,kj->prj', expected, columns, precision=high)  8.96 us
    dot_general x1, matrix products, local(): jnp.einsum('prk,kj->prj', closed, full_dyn, precision=high)  7.06 us
    dynamic_update_slice x9, local copies, waits for them, and re-layouts, gathered(): whole = lax.dynamic_update_slice_in_dim(whole, part, source * size, dim)  5.84 us
    dot_general x1, matrix products, local(): free_next = jnp.einsum('ij,pj->pi', full_dyn, state, precision=highest)  5.65 us
    pallas_call x1, Pallas kernels, leaf_sums(): pl.pallas_call(leaf_sum_kernel, grid=(rows // tile,), in_specs=[pl.BlockS...  5.03 us
  transfers between devices with their start and end apart: 16, of which 6 were waited for; matrix products, arithmetic and copies ran while one was open for 21% of the time, Pallas kernels for 9%

profile of v1, /device:TPU:0, one launch (start us, length us, event | category | flops | bytes accessed | tf_op | source)
XLA Modules:
  0.0 202.6 jit_solution(5582069538723956979)
XLA Ops:
  0.6 3.1 %collective-permute-start.2 = (f32[256,1024]{1,0:T(8,128)}, f32[256,1024]{1,0:T(8,128)}, u32[]{:S(2)}, u32[]{:S(2)}) collective-permute-start(f32[256,1024]{1,0:T(8,128)} %param.12), channel_id=1, source_target_pairs={{0,1},{1,2},{2,3},{3,0},{4,5},{5,6},{6,7},{7,4},{8,9},{9,10},{10,1... | collective-permute-start | bytes 3145736 | tf_op jit(solution)/shard_map/ppermute | solution.py:14
  3.7 2.1 %collective-permute-start.3 = (f32[256,1024]{1,0:T(8,128)}, f32[256,1024]{1,0:T(8,128)}, u32[]{:S(2)}, u32[]{:S(2)}) collective-permute-start(f32[256,1024]{1,0:T(8,128)} %param.12), channel_id=1, source_target_pairs={{0,3},{1,0},{2,1},{3,2},{4,7},{5,4},{6,5},{7,6},{8,11},{9,8},{10,9... | collective-permute-start | bytes 3145736 | tf_op jit(solution)/shard_map/ppermute | solution.py:14
  7.3 3.4 %copy-done = f32[8,256,1024]{2,1,0:T(8,128)S(1)} copy-done((f32[8,256,1024]{2,1,0:T(8,128)S(1)}, f32[8,256,1024]{2,1,0:T(8,128)}, u32[]{:S(2)}) %copy-start) | copy-done | bytes 8388632
  10.7 5.0 %shard_map.112 = (f32[1,256,1024]{2,1,0:T(8,128)S(1)}, f32[2,256,1024]{2,1,0:T(8,128)S(1)}, f32[1,256,1024]{2,1,0:T(8,128)}) custom-call(f32[8,4]{1,0:T(8,128)S(1)} %broadcast_select_fusion.member_ref, f32[8,256,1024]{2,1,0:T(8,128)S(1)} %copy-done), custom_call_target="tpu_custom_call" | custom-call | tf_op jit(solution)/shard_map/pallas_call | solution.py:62
  15.8 2.5 %collective-permute-start = (f32[1,256,1024]{2,1,0:T(8,128)}, f32[1,256,1024]{2,1,0:T(8,128)}, u32[]{:S(2)}, u32[]{:S(2)}) collective-permute-start(f32[1,256,1024]{2,1,0:T(8,128)} %get-tuple-element.7), channel_id=1, source_target_pairs={{0,4},{4,8},{8,12},{12,16},{16,20},{20,24},{24,28},{1,5},{5,9},{9,... | collective-permute-start | bytes 3145736 | tf_op jit(solution)/shard_map/ppermute | solution.py:155
  20.1 2.5 %broadcast_in_dim.112 = f32[1024,1024]{1,0:T(8,128)} broadcast(f32[]{:T(128)} %constant.39.clone.1), dimensions={} | broadcast | bytes 4194308 | tf_op jit(solution)/shard_map/broadcast_in_dim | solution.py:29
  23.6 28.0 %collective-permute-done.11 = f32[2,256]{1,0:T(2,128)S(1)} collective-permute-done((f32[2,256]{1,0:T(2,128)S(1)}, f32[2,256]{1,0:T(2,128)S(1)}, u32[]{:S(2)}, u32[]{:S(2)}) %collective-permute-start.11) | collective-permute-done | bytes 2080 | tf_op jit(solution)/shard_map/ppermute | solution.py:14
  56.0 3.7 %collective-permute-done.13 = f32[2,256]{1,0:T(2,128)S(1)} collective-permute-done((f32[2,256]{1,0:T(2,128)S(1)}, f32[2,256]{1,0:T(2,128)S(1)}, u32[]{:S(2)}, u32[]{:S(2)}) %collective-permute-start.13) | collective-permute-done | bytes 2080 | tf_op jit(solution)/shard_map/ppermute | solution.py:14
  60.5 2.1 %add_divide_fusion = f32[2,256,1024]{2,1,0:T(8,128)S(1)} fusion(f32[2,256,1024]{2,1,0:T(8,128)S(1)} %get-tuple-element.6, f32[1,256,1024]{2,1,0:T(8,128)} %collective-permute-done.1, f32[1,256,1024]{2,1,0:T(8,128)} %collective-permute-done, f32[2]{0:T(128)S(1)} %fusion.37), kind=kLoop, calls=%fused_computation.3 | loop fusion | flops 1572864 | bytes 6291464 | tf_op jit(solution)/shard_map/div | solution.py:159
  64.8 19.3 %collective-permute-start.8 = (f32[2,256,256]{2,1,0:T(8,128)S(1)}, f32[2,256,256]{2,1,0:T(8,128)S(1)}, u32[]{:S(2)}, u32[]{:S(2)}) collective-permute-start(f32[2,256,256]{2,1,0:T(8,128)S(1)} %get-tuple-element.16), channel_id=1, source_target_pairs={{0,1},{1,2},{2,3},{3,0},{4,5},{5,6},{6,7},{7,4},{8,9},{9,10},{10,1... | collective-permute-start | bytes 1572872 | tf_op jit(solution)/shard_map/ppermute | solution.py:14
  85.7 2.3 %constant_dynamic-update-slice_fusion.13 = f32[1024,1024]{1,0:T(8,128)} fusion(f32[1024,1024]{1,0:T(8,128)} %constant_dynamic-update-slice_fusion.14, f32[256,1024]{1,0:T(8,128)} %collective-permute-done.2, s32[]{:T(128)S(6)} %select_n.60), kind=kLoop, calls=%fused_computation.48 | loop fusion | bytes 2097156 | tf_op jit(solution)/shard_map/dynamic_update_slice | solution.py:33
  88.0 2.3 %constant_dynamic-update-slice_fusion.12 = f32[1024,1024]{1,0:T(8,128)} fusion(f32[1024,1024]{1,0:T(8,128)} %constant_dynamic-update-slice_fusion.13, f32[256,1024]{1,0:T(8,128)} %collective-permute-done.3, s32[]{:T(128)S(6)} %select_n.61), kind=kLoop, calls=%fused_computation.47 | loop fusion | bytes 2097156 | tf_op jit(solution)/shard_map/dynamic_update_slice | solution.py:33
  90.3 37.1 %collective-permute-done.4 = f32[256,1024]{1,0:T(8,128)S(1)} collective-permute-done((f32[256,1024]{1,0:T(8,128)}, f32[256,1024]{1,0:T(8,128)S(1)}, u32[]{:S(2)}, u32[]{:S(2)}) %collective-permute-start.4) | collective-permute-done | bytes 1048608 | tf_op jit(solution)/shard_map/ppermute | solution.py:14
  128.5 2.2 %fusion.11 = f32[2,256,256]{2,1,0:T(8,128)S(1)} fusion(f32[2,256,1024]{2,1,0:T(8,128)S(1)} %add_divide_fusion, f32[1024,1024]{1,0:T(8,128)} %constant_dynamic-update-slice_fusion.11, s32[]{:T(128)S(6)} %select_n.61), kind=kOutput, calls=%fused_computation.13 | convolution fusion | flops 805306368 | bytes 3670020 | tf_op jit(solution)/shard_map/prk,kj->prj/dot_general | solution.py:167
  130.7 2.2 %fusion.9 = f32[2,256,256]{2,1,0:T(8,128)S(1)} fusion(f32[2,256,1024]{2,1,0:T(8,128)S(1)} %add_divide_fusion, f32[1024,1024]{1,0:T(8,128)} %constant_dynamic-update-slice_fusion.11, s32[]{:T(128)S(6)} %select_n.60), kind=kOutput, calls=%fused_computation.11 | convolution fusion | flops 805306368 | bytes 3670020 | tf_op jit(solution)/shard_map/prk,kj->prj/dot_general | solution.py:167
  133.0 5.6 %fusion.40 = f32[2,1024]{1,0:T(2,128)S(1)} fusion(f32[2,1024]{1,0:T(2,128)S(1)} %constant_dynamic-update-slice_fusion, f32[1024,1024]{1,0:T(8,128)} %constant_dynamic-update-slice_fusion.11), kind=kOutput, calls=%fused_computation.68 | convolution fusion | flops 25165824 | bytes 4210688 | tf_op jit(solution)/shard_map/ij,pj->pi/dot_general | solution.py:180
  138.6 2.2 %fusion.7 = f32[2,256,256]{2,1,0:T(8,128)S(1)} fusion(f32[2,256,1024]{2,1,0:T(8,128)S(1)} %add_divide_fusion, f32[1024,1024]{1,0:T(8,128)} %constant_dynamic-update-slice_fusion.11, s32[]{:T(128)S(6)} %select_n.62), kind=kOutput, calls=%fused_computation.9 | convolution fusion | flops 805306368 | bytes 3670020 | tf_op jit(solution)/shard_map/prk,kj->prj/dot_general | solution.py:167
  142.1 3.0 %collective-permute-start.6 = (f32[2,256,256]{2,1,0:T(8,128)S(1)}, f32[2,256,256]{2,1,0:T(8,128)S(1)}, u32[]{:S(2)}, u32[]{:S(2)}) collective-permute-start(f32[2,256,256]{2,1,0:T(8,128)S(1)} %fusion.9), channel_id=1, source_target_pairs={{0,3},{1,0},{2,1},{3,2},{4,7},{5,4},{6,5},{7,6},{8,11},{9,8},{10,9... | collective-permute-start | bytes 1572872 | tf_op jit(solution)/shard_map/ppermute | solution.py:14
  145.2 2.2 %convolution_dynamic-update-slice_fusion = f32[2,1024,256]{2,1,0:T(8,128)S(1)} fusion(f32[2,1024,256]{2,1,0:T(8,128)S(1)} %broadcast.26.clone.1, s32[]{:T(128)S(6)} %select_n.59, f32[2,256,1024]{2,1,0:T(8,128)S(1)} %add_divide_fusion, f32[1024,1024]{1,0:T(8,128)} %constant_dynamic-update-slice_fusion.11), kind=kOutput, calls=%fused_computation.5 | convolution fusion | flops 805306368 | bytes 3671040 | tf_op jit(solution)/shard_map/prk,kj->prj/dot_general | solution.py:167
  148.0 13.2 %collective-permute-done.10 = f32[2,256,256]{2,1,0:T(8,128)S(1)} collective-permute-done((f32[2,256,256]{2,1,0:T(8,128)S(1)}, f32[2,256,256]{2,1,0:T(8,128)S(1)}, u32[]{:S(2)}, u32[]{:S(2)}) %collective-permute-start.10) | collective-permute-done | bytes 524320 | tf_op jit(solution)/shard_map/ppermute | solution.py:14
  161.2 2.3 %fusion.13 = f32[2,256,256]{1,2,0:T(8,128)S(1)} fusion(f32[2,1024,256]{2,1,0:T(8,128)S(1)} %constant_dynamic-update-slice_fusion.4.side_ref, f32[1024,1024]{1,0:T(8,128)} %constant_dynamic-update-slice_fusion.11, s32[]{:T(128)S(6)} %select_n.59), kind=kOutput, calls=%fused_computation.15 | convolution fusion | flops 805306368 | bytes 3670020 | tf_op jit(solution)/shard_map/kr,pka->pra/dot_general | solution.py:190
  164.8 13.8 %shard_map.113 = f32[2,256,256]{2,1,0:T(8,128)S(1)} custom-call(f32[256,256]{1,0:T(8,128)S(1)} %copy-done.2, f32[1024,256]{1,0:T(8,128)S(1)} %copy-done.1, f32[2,1024,256]{2,1,0:T(8,128)S(1)} %constant_dynamic-update-slice_fusion.4.side_ref), custom_call_target="tpu_custom_call" | custom-call | flops 20132659200 | bytes 4194304 | tf_op jit(solution)/shard_map/pallas_call | solution.py:110
  184.4 10.4 %collective-permute-done.7 = f32[2,256,256]{2,1,0:T(8,128)S(1)} collective-permute-done((f32[2,256,256]{2,1,0:T(8,128)S(1)}, f32[2,256,256]{2,1,0:T(8,128)S(1)}, u32[]{:S(2)}, u32[]{:S(2)}) %collective-permute-start.7) | collective-permute-done | bytes 524320 | tf_op jit(solution)/shard_map/ppermute | solution.py:14
  194.9 7.1 %fusion.2 = f32[2,256,1024]{2,1,0:T(8,128)} fusion(f32[1024,1024]{1,0:T(8,128)} %constant_dynamic-update-slice_fusion.11, f32[2,256,1024]{1,2,0:T(8,128)S(1)} %fusion.39, f32[2,1024,256]{2,1,0:T(8,128)S(1)} %constant_dynamic-update-slice_fusion.8, f32[256,1024]{1,0:T(8,128)S(1)} %copy-done.5), kind=kOutput, calls=%fused_computation.4 | convolution fusion | flops 3222274048 | bytes 11534336 | tf_op jit(solution)/shard_map/prk,kj->prj/dot_general | solution.py:198
  (71 shorter events, 23.9 us)
Async XLA Ops:
  0.6 83.5 %collective-permute-start.2 = (f32[256,1024]{1,0:T(8,128)}, f32[256,1024]{1,0:T(8,128)}, u32[]{:S(2)}, u32[]{:S(2)}) collective-permute-start(f32[256,1024]{1,0:T(8,128)} %param.12), channel_id=1, source_target_pairs={{0,1},{1,2},{2,3},{3,0},{4,5},{5,6},{6,7},{7,4},{8,9},{9,10},{10,1... | collective-permute-start | bytes 3145736 | tf_op jit(solution)/shard_map/ppermute | solution.py:14
  3.7 84.3 %collective-permute-start.3 = (f32[256,1024]{1,0:T(8,128)}, f32[256,1024]{1,0:T(8,128)}, u32[]{:S(2)}, u32[]{:S(2)}) collective-permute-start(f32[256,1024]{1,0:T(8,128)} %param.12), channel_id=1, source_target_pairs={{0,3},{1,0},{2,1},{3,2},{4,7},{5,4},{6,5},{7,6},{8,11},{9,8},{10,9... | collective-permute-start | bytes 3145736 | tf_op jit(solution)/shard_map/ppermute | solution.py:14
  7.3 3.4 %copy-start = (f32[8,256,1024]{2,1,0:T(8,128)S(1)}, f32[8,256,1024]{2,1,0:T(8,128)}, u32[]{:S(2)}) copy-start(f32[8,256,1024]{2,1,0:T(8,128)} %leaf_ref.1) | copy-start | bytes 25165828
  10.7 8.8 %copy-start.7 = (f32[2,256]{1,0:T(2,128)S(1)}, f32[2,256]{1,0:T(2,128)}, u32[]{:S(2)}) copy-start(f32[2,256]{1,0:T(2,128)} %param.16) | copy-start | bytes 6148
  10.7 9.2 %copy-start.8 = (s32[64]{0:T(128)S(1)}, s32[64]{0:T(128)}, u32[]{:S(2)}) copy-start(s32[64]{0:T(128)} %param.14) | copy-start | bytes 772
  15.8 44.8 %collective-permute-start = (f32[1,256,1024]{2,1,0:T(8,128)}, f32[1,256,1024]{2,1,0:T(8,128)}, u32[]{:S(2)}, u32[]{:S(2)}) collective-permute-start(f32[1,256,1024]{2,1,0:T(8,128)} %get-tuple-element.7), channel_id=1, source_target_pairs={{0,4},{4,8},{8,12},{12,16},{16,20},{20,24},{24,28},{1,5},{5,9},{9,... | collective-permute-start | bytes 3145736 | tf_op jit(solution)/shard_map/ppermute | solution.py:155
  18.2 42.3 %collective-permute-start.1 = (f32[1,256,1024]{2,1,0:T(8,128)S(1)}, f32[1,256,1024]{2,1,0:T(8,128)}, u32[]{:S(2)}, u32[]{:S(2)}) collective-permute-start(f32[1,256,1024]{2,1,0:T(8,128)S(1)} %get-tuple-element.8), channel_id=1, source_target_pairs={{4,0},{8,4},{12,8},{16,12},{20,16},{24,20},{28,24},{5,1},{9,5},{13... | collective-permute-start | bytes 3145736 | tf_op jit(solution)/shard_map/ppermute | solution.py:156
  19.5 32.2 %collective-permute-start.11 = (f32[2,256]{1,0:T(2,128)S(1)}, f32[2,256]{1,0:T(2,128)S(1)}, u32[]{:S(2)}, u32[]{:S(2)}) collective-permute-start(f32[2,256]{1,0:T(2,128)S(1)} %copy-done.7), channel_id=1, source_target_pairs={{0,1},{1,2},{2,3},{3,0},{4,5},{5,6},{6,7},{7,4},{8,9},{9,10},{10,1... | collective-permute-start | bytes 6152 | tf_op jit(solution)/shard_map/ppermute | solution.py:14
  20.1 2.5 %copy-start.4 = (f32[256,1024]{1,0:T(8,128)S(1)}, f32[256,1024]{1,0:T(8,128)}, u32[]{:S(2)}) copy-start(f32[256,1024]{1,0:T(8,128)} %param.12) | copy-start | bytes 3145732
  51.7 3.6 %collective-permute-start.12 = (f32[2,256]{1,0:T(2,128)S(1)}, f32[2,256]{1,0:T(2,128)S(1)}, u32[]{:S(2)}, u32[]{:S(2)}) collective-permute-start(f32[2,256]{1,0:T(2,128)S(1)} %copy-done.7), channel_id=1, source_target_pairs={{0,3},{1,0},{2,1},{3,2},{4,7},{5,4},{6,5},{7,6},{8,11},{9,8},{10,9... | collective-permute-start | bytes 6152 | tf_op jit(solution)/shard_map/ppermute | solution.py:14
  55.3 4.5 %collective-permute-start.13 = (f32[2,256]{1,0:T(2,128)S(1)}, f32[2,256]{1,0:T(2,128)S(1)}, u32[]{:S(2)}, u32[]{:S(2)}) collective-permute-start(f32[2,256]{1,0:T(2,128)S(1)} %copy-done.7), channel_id=1, source_target_pairs={{0,2},{1,3},{2,0},{3,1},{4,6},{5,7},{6,4},{7,5},{8,10},{9,11},{10,... | collective-permute-start | bytes 6152 | tf_op jit(solution)/shard_map/ppermute | solution.py:14
  59.8 67.7 %collective-permute-start.4 = (f32[256,1024]{1,0:T(8,128)}, f32[256,1024]{1,0:T(8,128)S(1)}, u32[]{:S(2)}, u32[]{:S(2)}) collective-permute-start(f32[256,1024]{1,0:T(8,128)} %param.12), channel_id=1, source_target_pairs={{0,2},{1,3},{2,0},{3,1},{4,6},{5,7},{6,4},{7,5},{8,10},{9,11},{10,... | collective-permute-start | bytes 3145736 | tf_op jit(solution)/shard_map/ppermute | solution.py:14
  62.6 1.2 copy-start.1
  64.8 82.6 %collective-permute-start.8 = (f32[2,256,256]{2,1,0:T(8,128)S(1)}, f32[2,256,256]{2,1,0:T(8,128)S(1)}, u32[]{:S(2)}, u32[]{:S(2)}) collective-permute-start(f32[2,256,256]{2,1,0:T(8,128)S(1)} %get-tuple-element.16), channel_id=1, source_target_pairs={{0,1},{1,2},{2,3},{3,0},{4,5},{5,6},{6,7},{7,4},{8,9},{9,10},{10,1... | collective-permute-start | bytes 1572872 | tf_op jit(solution)/shard_map/ppermute | solution.py:14
  84.2 63.7 %collective-permute-start.9 = (f32[2,256,256]{2,1,0:T(8,128)S(1)}, f32[2,256,256]{2,1,0:T(8,128)S(1)}, u32[]{:S(2)}, u32[]{:S(2)}) collective-permute-start(f32[2,256,256]{2,1,0:T(8,128)S(1)} %get-tuple-element.16), channel_id=1, source_target_pairs={{0,3},{1,0},{2,1},{3,2},{4,7},{5,4},{6,5},{7,6},{8,11},{9,8},{10,9... | collective-permute-start | bytes 1572872 | tf_op jit(solution)/shard_map/ppermute | solution.py:14
  84.2 77.0 %collective-permute-start.10 = (f32[2,256,256]{2,1,0:T(8,128)S(1)}, f32[2,256,256]{2,1,0:T(8,128)S(1)}, u32[]{:S(2)}, u32[]{:S(2)}) collective-permute-start(f32[2,256,256]{2,1,0:T(8,128)S(1)} %get-tuple-element.16), channel_id=1, source_target_pairs={{0,2},{1,3},{2,0},{3,1},{4,6},{5,7},{6,4},{7,5},{8,10},{9,11},{10,... | collective-permute-start | bytes 1572872 | tf_op jit(solution)/shard_map/ppermute | solution.py:14
  140.9 42.4 %collective-permute-start.5 = (f32[2,256,256]{2,1,0:T(8,128)S(1)}, f32[2,256,256]{2,1,0:T(8,128)S(1)}, u32[]{:S(2)}, u32[]{:S(2)}) collective-permute-start(f32[2,256,256]{2,1,0:T(8,128)S(1)} %fusion.11), channel_id=1, source_target_pairs={{0,1},{1,2},{2,3},{3,0},{4,5},{5,6},{6,7},{7,4},{8,9},{9,10},{10,1... | collective-permute-start | bytes 1572872 | tf_op jit(solution)/shard_map/ppermute | solution.py:14
  142.1 41.2 %collective-permute-start.6 = (f32[2,256,256]{2,1,0:T(8,128)S(1)}, f32[2,256,256]{2,1,0:T(8,128)S(1)}, u32[]{:S(2)}, u32[]{:S(2)}) collective-permute-start(f32[2,256,256]{2,1,0:T(8,128)S(1)} %fusion.9), channel_id=1, source_target_pairs={{0,3},{1,0},{2,1},{3,2},{4,7},{5,4},{6,5},{7,6},{8,11},{9,8},{10,9... | collective-permute-start | bytes 1572872 | tf_op jit(solution)/shard_map/ppermute | solution.py:14
  147.5 47.3 %collective-permute-start.7 = (f32[2,256,256]{2,1,0:T(8,128)S(1)}, f32[2,256,256]{2,1,0:T(8,128)S(1)}, u32[]{:S(2)}, u32[]{:S(2)}) collective-permute-start(f32[2,256,256]{2,1,0:T(8,128)S(1)} %fusion.7), channel_id=1, source_target_pairs={{0,2},{1,3},{2,0},{3,1},{4,6},{5,7},{6,4},{7,5},{8,10},{9,11},{10,... | collective-permute-start | bytes 1572872 | tf_op jit(solution)/shard_map/ppermute | solution.py:14
  161.2 3.5 %copy-start.2 = (f32[256,256]{1,0:T(8,128)S(1)}, f32[256,256]{1,0:T(8,128)}, u32[]{:S(2)}) copy-start(f32[256,256]{1,0:T(8,128)} %cost_ref.1) | copy-start | bytes 786436
  179.5 22.4 %collective-permute-start.14 = (f32[1,256]{1,0:T(1,128)S(1)}, f32[1,256]{1,0:T(1,128)S(1)}, u32[]{:S(2)}, u32[]{:S(2)}) collective-permute-start(f32[1,256]{1,0:T(1,128)S(1)} %get-tuple-element.13), channel_id=1, source_target_pairs={{0,4},{4,8},{8,12},{12,16},{16,20},{20,24},{24,28},{1,5},{5,9},{9,... | collective-permute-start | bytes 3080 | tf_op jit(solution)/shard_map/ppermute | solution.py:187
  181.3 20.6 %collective-permute-start.15 = (f32[1,256]{1,0:T(1,128)S(1)}, f32[1,256]{1,0:T(1,128)S(1)}, u32[]{:S(2)}, u32[]{:S(2)}) collective-permute-start(f32[1,256]{1,0:T(1,128)S(1)} %get-tuple-element.14), channel_id=1, source_target_pairs={{4,0},{8,4},{12,8},{16,12},{20,16},{24,20},{28,24},{5,1},{9,5},{13... | collective-permute-start | bytes 3080 | tf_op jit(solution)/shard_map/ppermute | solution.py:188
  183.4 11.5 %copy-start.5 = (f32[256,1024]{1,0:T(8,128)S(1)}, f32[256,1024]{1,0:T(8,128)}, u32[]{:S(2)}) copy-start(f32[256,1024]{1,0:T(8,128)} %param.10) | copy-start | bytes 3145732
  194.9 7.1 %copy-start.6 = (f32[8,256]{1,0:T(8,128)S(1)}, f32[8,256]{1,0:T(8,128)}, u32[]{:S(2)}) copy-start(f32[8,256]{1,0:T(8,128)} %param.17) | copy-start | bytes 24580
  (1 other events, 1.2 us)

commit v2 on v1

--- a/solution.py
+++ b/solution.py
@@ -31,6 +31,35 @@
     for step, part in parts:
         source = lax.rem(me + count - step, count)
         whole = lax.dynamic_update_slice_in_dim(whole, part, source * size, dim)
+    return whole
+
+
+def gathered_once(block):
+    leaves, count = lax.axis_size("leaf"), lax.axis_size("mat")
+    size = block.shape[0]
+    if leaves % 4 or size % 32:
+        return gathered(block, "mat", 0)
+    half, quarter = leaves // 2, size // 4
+    leaf, me = lax.axis_index("leaf"), lax.axis_index("mat")
+    upper, core = leaf // half, lax.rem(leaf, 2)
+    across = [(i, (i + half) % leaves) for i in range(leaves)]
+    beside = [(i, i ^ 1) for i in range(leaves)]
+    mine = lax.dynamic_slice_in_dim(block, (2 * upper + core) * quarter, quarter, 0)
+    own = [(step, shifted(mine, "mat", step)) for step in shifts_of(count)]
+    shape = (size * count,) + block.shape[1:]
+    whole = lax.dynamic_update_slice_in_dim(jnp.zeros(shape, block.dtype), block, me * size, 0)
+    for step, part in own:
+        start = lax.rem(me + count - step, count) * size
+        other = lax.ppermute(part, "leaf", across)
+        pieces = (
+            (part, upper, core),
+            (other, 1 - upper, core),
+            (lax.ppermute(part, "leaf", beside), upper, 1 - core),
+            (lax.ppermute(other, "leaf", beside), 1 - upper, 1 - core),
+        )
+        for piece, high_half, side in pieces:
+            at = start + (2 * high_half + side) * quarter
+            whole = lax.dynamic_update_slice_in_dim(whole, piece, at, 0)
     return whole
 
 
@@ -139,7 +168,7 @@
     count = lax.axis_size("mat")
     forward, backward = edge_rows(parent_state)
     row_start = column * slab_rows
-    full_dyn = gathered(dynamics, "mat", 0)
+    full_dyn = gathered_once(dynamics)
     weights = prob_weight.astype(jnp.float32)
     my_parents = lax.dynamic_slice_in_dim(parent_of, leaf_index * leaf_dev, leaf_dev, 0)
     my_weights = lax.dynamic_slice_in_dim(weights, leaf_index * leaf_dev, leaf_dev, 0)
@@ -191,11 +220,15 @@
     gain_rows = -jnp.einsum("pra,pab->prb", coupling_rows, inv, precision=high)
     feedback = jnp.einsum("prb,pkb->prk", gain_rows, side, precision=high)
 
-    for step, part in parts:
+    for step, part in parts[:-1]:
         source = lax.rem(column + count - step, count)
         value_cols = lax.dynamic_update_slice_in_dim(value_cols, part, source * slab_rows, 1)
     closed = jnp.swapaxes(value_cols, 1, 2) + feedback
     new_value = section_cost[None] + jnp.einsum("prk,kj->prj", closed, full_dyn, precision=high)
+    for step, part in parts[-1:]:
+        source = lax.rem(column + count - step, count)
+        rows = lax.dynamic_slice_in_dim(full_dyn, source * slab_rows, slab_rows, 0)
+        new_value = new_value + jnp.einsum("pkr,kj->prj", part, rows, precision=high)
 
     extended = jnp.concatenate([below, following, above], axis=0)
     child_state = disturbance

time: 203 us -> 189 us (0.931)
  the two profiles are of different devices: /device:TPU:0 before, /device:TPU:2 now
where the time goes in v2:
time: 189 us; the launch traced here: 188 us
  waiting for transfers between devices  67.9 us (36%)
  starting transfers between devices  49.7 us (26%)
  matrix products  30.7 us (16%)
  local copies, waits for them, and re-layouts  18.7 us (10%)
  Pallas kernels  17.5 us (9%)
  other arithmetic  2.96 us (2%)
    ppermute x12, waiting for transfers between devices, shifted(): lax.ppermute(block, axis, [(i, (i + step) % count) for i in range(count)])  51.2 us
    ppermute x12, starting transfers between devices, shifted(): lax.ppermute(block, axis, [(i, (i + step) % count) for i in range(count)])  23.7 us
    ppermute x3, waiting for transfers between devices, gathered_once(): other = lax.ppermute(part, 'leaf', across)  16.7 us
    pallas_call x1, Pallas kernels, inverses(): pl.pallas_call(inverse_kernel, in_specs=[pl.BlockSpec(memory_space=pltpu....  13.8 us
    ppermute x1, starting transfers between devices, local(): from_high = lax.ppermute(low, 'leaf', backward)  12.9 us
    dot_general x4, matrix products, value_block(): return jnp.einsum('prk,kj->prj', expected, columns, precision=high)  8.91 us
    dynamic_update_slice x12, local copies, waits for them, and re-layouts, gathered_once(): whole = lax.dynamic_update_slice_in_dim(whole, piece, at, 0)  8.6 us
    dot_general x1, matrix products, local(): jnp.einsum('prk,kj->prj', closed, full_dyn, precision=high)  7.18 us
  transfers between devices with their start and end apart: 25, of which 6 were waited for; matrix products, arithmetic and copies ran while one was open for 24% of the time, Pallas kernels for 9%

profile of v2, /device:TPU:2, one launch (start us, length us, event | category | flops | bytes accessed | tf_op | source)
XLA Modules:
  0.0 188.5 jit_solution(6377225568094716183)
XLA Ops:
  3.3 2.2 %collective-permute-start.6 = (f32[64,1024]{1,0:T(8,128)S(1)}, f32[64,1024]{1,0:T(8,128)S(1)}, u32[]{:S(2)}, u32[]{:S(2)}) collective-permute-start(f32[64,1024]{1,0:T(8,128)S(1)} %constant_dynamic-slice_fusion.1), channel_id=1, source_target_pairs={{0,3},{1,0},{2,1},{3,2},{4,7},{5,4},{6,5},{7,6},{8,11},{9,8},{10,9... | collective-permute-start | bytes 786440 | tf_op jit(solution)/shard_map/ppermute | solution.py:14
  7.9 2.2 %collective-permute-start.21 = (f32[2,256]{1,0:T(2,128)}, f32[2,256]{1,0:T(2,128)S(1)}, u32[]{:S(2)}, u32[]{:S(2)}) collective-permute-start(f32[2,256]{1,0:T(2,128)} %param.16), channel_id=1, source_target_pairs={{0,3},{1,0},{2,1},{3,2},{4,7},{5,4},{6,5},{7,6},{8,11},{9,8},{10,9... | collective-permute-start | bytes 6152 | tf_op jit(solution)/shard_map/ppermute | solution.py:14
  11.8 2.5 %broadcast_in_dim.112 = f32[1024,1024]{1,0:T(8,128)} broadcast(f32[]{:T(128)} %constant.51.clone.1), dimensions={} | broadcast | bytes 4194308 | tf_op jit(solution)/shard_map/broadcast_in_dim | solution.py:50
  15.8 3.4 %copy-done = f32[8,256,1024]{2,1,0:T(8,128)S(1)} copy-done((f32[8,256,1024]{2,1,0:T(8,128)S(1)}, f32[8,256,1024]{2,1,0:T(8,128)}, u32[]{:S(2)}) %copy-start) | copy-done | bytes 8388632
  19.2 3.7 %shard_map.112 = (f32[1,256,1024]{2,1,0:T(8,128)S(1)}, f32[2,256,1024]{2,1,0:T(8,128)S(1)}, f32[1,256,1024]{2,1,0:T(8,128)S(1)}) custom-call(f32[8,4]{1,0:T(8,128)S(1)} %broadcast_select_fusion.member_ref, f32[8,256,1024]{2,1,0:T(8,128)S(1)} %copy-done), custom_call_target="tpu_custom_call" | custom-call | tf_op jit(solution)/shard_map/pallas_call | solution.py:91
  23.0 6.3 %collective-permute-start.22 = (f32[2,256]{1,0:T(2,128)S(1)}, f32[2,256]{1,0:T(2,128)S(1)}, u32[]{:S(2)}, u32[]{:S(2)}) collective-permute-start(f32[2,256]{1,0:T(2,128)S(1)} %copy-done.7), channel_id=1, source_target_pairs={{0,2},{1,3},{2,0},{3,1},{4,6},{5,7},{6,4},{7,5},{8,10},{9,11},{10,... | collective-permute-start | bytes 6152 | tf_op jit(solution)/shard_map/ppermute | solution.py:14
  33.4 2.4 %collective-permute-done.3 = f32[64,1024]{1,0:T(8,128)S(1)} collective-permute-done((f32[64,1024]{1,0:T(8,128)S(1)}, f32[64,1024]{1,0:T(8,128)S(1)}, u32[]{:S(2)}, u32[]{:S(2)}) %collective-permute-start.3) | collective-permute-done | bytes 262176 | tf_op jit(solution)/shard_map/ppermute | solution.py:53
  37.3 12.9 %collective-permute-start.1 = (f32[1,256,1024]{2,1,0:T(8,128)S(1)}, f32[1,256,1024]{2,1,0:T(8,128)S(1)}, u32[]{:S(2)}, u32[]{:S(2)}) collective-permute-start(f32[1,256,1024]{2,1,0:T(8,128)S(1)} %get-tuple-element.8), channel_id=1, source_target_pairs={{4,0},{8,4},{12,8},{16,12},{20,16},{24,20},{28,24},{5,1},{9,5},{13... | collective-permute-start | bytes 3145736 | tf_op jit(solution)/shard_map/ppermute | solution.py:185
  50.9 2.6 %collective-permute-start.11 = (f32[64,1024]{1,0:T(8,128)S(1)}, f32[64,1024]{1,0:T(8,128)S(1)}, u32[]{:S(2)}, u32[]{:S(2)}) collective-permute-start(f32[64,1024]{1,0:T(8,128)S(1)} %collective-permute-done.10), channel_id=1, source_target_pairs={{0,16},{4,20},{8,24},{12,28},{16,0},{20,4},{24,8},{28,12},{1,17},{... | collective-permute-start | bytes 786440 | tf_op jit(solution)/shard_map/ppermute | solution.py:53
  56.2 14.2 %collective-permute-done.11 = f32[64,1024]{1,0:T(8,128)S(1)} collective-permute-done((f32[64,1024]{1,0:T(8,128)S(1)}, f32[64,1024]{1,0:T(8,128)S(1)}, u32[]{:S(2)}, u32[]{:S(2)}) %collective-permute-start.11) | collective-permute-done | bytes 262176 | tf_op jit(solution)/shard_map/ppermute | solution.py:53
  74.8 5.6 %fusion.43 = f32[2,1024]{1,0:T(2,128)S(1)} fusion(f32[2,1024]{1,0:T(2,128)S(1)} %constant_dynamic-update-slice_fusion, f32[1024,1024]{1,0:T(8,128)} %constant_dynamic-update-slice_fusion.10), kind=kOutput, calls=%fused_computation.81 | convolution fusion | flops 25165824 | bytes 4210688 | tf_op jit(solution)/shard_map/ij,pj->pi/dot_general | solution.py:209
  83.4 3.8 %collective-permute-start.17 = (f32[2,256,256]{2,1,0:T(8,128)S(1)}, f32[2,256,256]{2,1,0:T(8,128)S(1)}, u32[]{:S(2)}, u32[]{:S(2)}) collective-permute-start(f32[2,256,256]{2,1,0:T(8,128)S(1)} %get-tuple-element.16), channel_id=1, source_target_pairs={{0,3},{1,0},{2,1},{3,2},{4,7},{5,4},{6,5},{7,6},{8,11},{9,8},{10,9... | collective-permute-start | bytes 1572872 | tf_op jit(solution)/shard_map/ppermute | solution.py:14
  89.4 2.2 %fusion.10 = f32[2,256,256]{2,1,0:T(8,128)S(1)} fusion(f32[2,256,1024]{2,1,0:T(8,128)S(1)} %add_divide_fusion, f32[1024,1024]{1,0:T(8,128)} %constant_dynamic-update-slice_fusion.10, s32[]{:T(128)S(6)} %select_n.116), kind=kOutput, calls=%fused_computation.13 | convolution fusion | flops 805306368 | bytes 3670020 | tf_op jit(solution)/shard_map/prk,kj->prj/dot_general | solution.py:196
  91.7 2.2 %fusion.6 = f32[2,256,256]{2,1,0:T(8,128)S(1)} fusion(f32[2,256,1024]{2,1,0:T(8,128)S(1)} %add_divide_fusion, f32[1024,1024]{1,0:T(8,128)} %constant_dynamic-update-slice_fusion.10, s32[]{:T(128)S(6)} %select_n.117), kind=kOutput, calls=%fused_computation.9 | convolution fusion | flops 805306368 | bytes 3670020 | tf_op jit(solution)/shard_map/prk,kj->prj/dot_general | solution.py:196
  94.5 3.3 %collective-permute-start.15 = (f32[2,256,256]{2,1,0:T(8,128)S(1)}, f32[2,256,256]{2,1,0:T(8,128)S(1)}, u32[]{:S(2)}, u32[]{:S(2)}) collective-permute-start(f32[2,256,256]{2,1,0:T(8,128)S(1)} %fusion.10), channel_id=1, source_target_pairs={{0,3},{1,0},{2,1},{3,2},{4,7},{5,4},{6,5},{7,6},{8,11},{9,8},{10,9... | collective-permute-start | bytes 1572872 | tf_op jit(solution)/shard_map/ppermute | solution.py:14
  97.9 2.2 %convolution_dynamic-update-slice_fusion = f32[2,1024,256]{2,1,0:T(8,128)S(1)} fusion(f32[2,1024,256]{2,1,0:T(8,128)S(1)} %broadcast.28.clone.1, s32[]{:T(128)S(6)} %select_n.100, f32[2,256,1024]{2,1,0:T(8,128)S(1)} %add_divide_fusion, f32[1024,1024]{1,0:T(8,128)} %constant_dynamic-update-slice_fusion.10), kind=kOutput, calls=%fused_computation.5 | convolution fusion | flops 805306368 | bytes 3671040 | tf_op jit(solution)/shard_map/prk,kj->prj/dot_general | solution.py:196
  101.4 9.4 %collective-permute-done.17 = f32[2,256,256]{2,1,0:T(8,128)S(1)} collective-permute-done((f32[2,256,256]{2,1,0:T(8,128)S(1)}, f32[2,256,256]{2,1,0:T(8,128)S(1)}, u32[]{:S(2)}, u32[]{:S(2)}) %collective-permute-start.17) | collective-permute-done | bytes 524320 | tf_op jit(solution)/shard_map/ppermute | solution.py:14
  110.9 32.8 %collective-permute-done.18 = f32[2,256,256]{2,1,0:T(8,128)S(1)} collective-permute-done((f32[2,256,256]{2,1,0:T(8,128)S(1)}, f32[2,256,256]{2,1,0:T(8,128)S(1)}, u32[]{:S(2)}, u32[]{:S(2)}) %collective-permute-start.18) | collective-permute-done | bytes 524320 | tf_op jit(solution)/shard_map/ppermute | solution.py:14
  144.9 13.8 %shard_map.113 = f32[2,256,256]{2,1,0:T(8,128)S(1)} custom-call(f32[256,256]{1,0:T(8,128)S(1)} %copy-done.2, f32[1024,256]{1,0:T(8,128)S(1)} %copy-done.1, f32[2,1024,256]{2,1,0:T(8,128)S(1)} %constant_dynamic-update-slice_fusion.4.side_ref), custom_call_target="tpu_custom_call" | custom-call | flops 20132659200 | bytes 4194304 | tf_op jit(solution)/shard_map/pallas_call | solution.py:139
  161.6 3.9 %collective-permute-start.24 = (f32[1,256]{1,0:T(1,128)S(1)}, f32[1,256]{1,0:T(1,128)S(1)}, u32[]{:S(2)}, u32[]{:S(2)}) collective-permute-start(f32[1,256]{1,0:T(1,128)S(1)} %get-tuple-element.14), channel_id=1, source_target_pairs={{4,0},{8,4},{12,8},{16,12},{20,16},{24,20},{28,24},{5,1},{9,5},{13... | collective-permute-start | bytes 3080 | tf_op jit(solution)/shard_map/ppermute | solution.py:217
  165.5 2.3 %fusion.14 = f32[2,256,256]{1,2,0:T(8,128)S(1)} fusion(f32[2,1024,256]{2,1,0:T(8,128)S(1)} %constant_dynamic-update-slice_fusion.4.side_ref, f32[1024,1024]{1,0:T(8,128)} %constant_dynamic-update-slice_fusion.10, s32[]{:T(128)S(6)} %select_n.100), kind=kOutput, calls=%fused_computation.17 | convolution fusion | flops 805306368 | bytes 3670020 | tf_op jit(solution)/shard_map/kr,pka->pra/dot_general | solution.py:219
  167.7 8.8 %collective-permute-done.19 = f32[2,256,256]{2,1,0:T(8,128)S(1)} collective-permute-done((f32[2,256,256]{2,1,0:T(8,128)S(1)}, f32[2,256,256]{2,1,0:T(8,128)S(1)}, u32[]{:S(2)}, u32[]{:S(2)}) %collective-permute-start.19) | collective-permute-done | bytes 524320 | tf_op jit(solution)/shard_map/ppermute | solution.py:14
  176.5 2.3 %fusion.4 = f32[2,256,1024]{2,1,0:T(8,128)S(1)} fusion(f32[2,256,256]{2,1,0:T(8,128)S(1)} %collective-permute-done.19, f32[1024,1024]{1,0:T(8,128)} %constant_dynamic-update-slice_fusion.10, s32[]{:T(128)S(6)} %select_n.117), kind=kOutput, calls=%fused_computation.7 | convolution fusion | flops 805306368 | bytes 3670020 | tf_op jit(solution)/shard_map/pkr,kj->prj/dot_general | solution.py:231
  180.6 7.2 %add_add_fusion = f32[2,256,1024]{2,1,0:T(8,128)} fusion(f32[2,256,1024]{2,1,0:T(8,128)S(1)} %fusion.4, f32[1024,1024]{1,0:T(8,128)} %constant_dynamic-update-slice_fusion.10, f32[2,256,1024]{1,2,0:T(8,128)S(1)} %fusion.42, f32[2,1024,256]{2,1,0:T(8,128)S(1)} %constant_dynamic-update-slice_fusion.8, f32[256,1024]{1,0:T(8,128)S(1)} %copy-done.5), kind=kOutput, calls=%fused_computation.3 | convolution fusion | flops 3222798336 | bytes 13631488 | tf_op jit(solution)/shard_map/prk,kj->prj/dot_general | solution.py:227
  (99 shorter events, 35.1 us)
Async XLA Ops:
  1.6 27.7 %collective-permute-start.2 = (f32[64,1024]{1,0:T(8,128)S(1)}, f32[64,1024]{1,0:T(8,128)S(1)}, u32[]{:S(2)}, u32[]{:S(2)}) collective-permute-start(f32[64,1024]{1,0:T(8,128)S(1)} %constant_dynamic-slice_fusion.1), channel_id=1, source_target_pairs={{0,1},{1,2},{2,3},{3,0},{4,5},{5,6},{6,7},{7,4},{8,9},{9,10},{10,1... | collective-permute-start | bytes 786440 | tf_op jit(solution)/shard_map/ppermute | solution.py:14
  3.3 30.2 %collective-permute-start.6 = (f32[64,1024]{1,0:T(8,128)S(1)}, f32[64,1024]{1,0:T(8,128)S(1)}, u32[]{:S(2)}, u32[]{:S(2)}) collective-permute-start(f32[64,1024]{1,0:T(8,128)S(1)} %constant_dynamic-slice_fusion.1), channel_id=1, source_target_pairs={{0,3},{1,0},{2,1},{3,2},{4,7},{5,4},{6,5},{7,6},{8,11},{9,8},{10,9... | collective-permute-start | bytes 786440 | tf_op jit(solution)/shard_map/ppermute | solution.py:14
  5.5 45.4 %collective-permute-start.10 = (f32[64,1024]{1,0:T(8,128)S(1)}, f32[64,1024]{1,0:T(8,128)S(1)}, u32[]{:S(2)}, u32[]{:S(2)}) collective-permute-start(f32[64,1024]{1,0:T(8,128)S(1)} %constant_dynamic-slice_fusion.1), channel_id=1, source_target_pairs={{0,2},{1,3},{2,0},{3,1},{4,6},{5,7},{6,4},{7,5},{8,10},{9,11},{10,... | collective-permute-start | bytes 786440 | tf_op jit(solution)/shard_map/ppermute | solution.py:14
  6.3 16.7 %collective-permute-start.20 = (f32[2,256]{1,0:T(2,128)}, f32[2,256]{1,0:T(2,128)S(1)}, u32[]{:S(2)}, u32[]{:S(2)}) collective-permute-start(f32[2,256]{1,0:T(2,128)} %param.16), channel_id=1, source_target_pairs={{0,1},{1,2},{2,3},{3,0},{4,5},{5,6},{6,7},{7,4},{8,9},{9,10},{10,1... | collective-permute-start | bytes 6152 | tf_op jit(solution)/shard_map/ppermute | solution.py:14
  7.9 22.9 %collective-permute-start.21 = (f32[2,256]{1,0:T(2,128)}, f32[2,256]{1,0:T(2,128)S(1)}, u32[]{:S(2)}, u32[]{:S(2)}) collective-permute-start(f32[2,256]{1,0:T(2,128)} %param.16), channel_id=1, source_target_pairs={{0,3},{1,0},{2,1},{3,2},{4,7},{5,4},{6,5},{7,6},{8,11},{9,8},{10,9... | collective-permute-start | bytes 6152 | tf_op jit(solution)/shard_map/ppermute | solution.py:14
  23.0 9.7 %collective-permute-start.22 = (f32[2,256]{1,0:T(2,128)S(1)}, f32[2,256]{1,0:T(2,128)S(1)}, u32[]{:S(2)}, u32[]{:S(2)}) collective-permute-start(f32[2,256]{1,0:T(2,128)S(1)} %copy-done.7), channel_id=1, source_target_pairs={{0,2},{1,3},{2,0},{3,1},{4,6},{5,7},{6,4},{7,5},{8,10},{9,11},{10,... | collective-permute-start | bytes 6152 | tf_op jit(solution)/shard_map/ppermute | solution.py:14
  29.3 6.6 %collective-permute-start.3 = (f32[64,1024]{1,0:T(8,128)S(1)}, f32[64,1024]{1,0:T(8,128)S(1)}, u32[]{:S(2)}, u32[]{:S(2)}) collective-permute-start(f32[64,1024]{1,0:T(8,128)S(1)} %collective-permute-done.2), channel_id=1, source_target_pairs={{0,16},{4,20},{8,24},{12,28},{16,0},{20,4},{24,8},{28,12},{1,17},{... | collective-permute-start | bytes 786440 | tf_op jit(solution)/shard_map/ppermute | solution.py:53
  30.8 49.7 %collective-permute-start = (f32[1,256,1024]{2,1,0:T(8,128)S(1)}, f32[1,256,1024]{2,1,0:T(8,128)S(1)}, u32[]{:S(2)}, u32[]{:S(2)}) collective-permute-start(f32[1,256,1024]{2,1,0:T(8,128)S(1)} %get-tuple-element.7), channel_id=1, source_target_pairs={{0,4},{4,8},{8,12},{12,16},{16,20},{20,24},{24,28},{1,5},{5,9},{9,... | collective-permute-start | bytes 3145736 | tf_op jit(solution)/shard_map/ppermute | solution.py:184
  32.8 4.5 %collective-permute-start.4 = (f32[64,1024]{1,0:T(8,128)S(1)}, f32[64,1024]{1,0:T(8,128)S(1)}, u32[]{:S(2)}, u32[]{:S(2)}) collective-permute-start(f32[64,1024]{1,0:T(8,128)S(1)} %collective-permute-done.2), channel_id=1, source_target_pairs={{0,4},{4,0},{8,12},{12,8},{16,20},{20,16},{24,28},{28,24},{1,5},{5... | collective-permute-start | bytes 786440 | tf_op jit(solution)/shard_map/ppermute | solution.py:57
  33.4 17.5 %collective-permute-start.7 = (f32[64,1024]{1,0:T(8,128)S(1)}, f32[64,1024]{1,0:T(8,128)S(1)}, u32[]{:S(2)}, u32[]{:S(2)}) collective-permute-start(f32[64,1024]{1,0:T(8,128)S(1)} %collective-permute-done.6), channel_id=1, source_target_pairs={{0,16},{4,20},{8,24},{12,28},{16,0},{20,4},{24,8},{28,12},{1,17},{... | collective-permute-start | bytes 786440 | tf_op jit(solution)/shard_map/ppermute | solution.py:53
  35.9 17.7 %collective-permute-start.5 = (f32[64,1024]{1,0:T(8,128)S(1)}, f32[64,1024]{1,0:T(8,128)S(1)}, u32[]{:S(2)}, u32[]{:S(2)}) collective-permute-start(f32[64,1024]{1,0:T(8,128)S(1)} %collective-permute-done.3), channel_id=1, source_target_pairs={{0,4},{4,0},{8,12},{12,8},{16,20},{20,16},{24,28},{28,24},{1,5},{5... | collective-permute-start | bytes 786440 | tf_op jit(solution)/shard_map/ppermute | solution.py:58
  37.3 43.2 %collective-permute-start.1 = (f32[1,256,1024]{2,1,0:T(8,128)S(1)}, f32[1,256,1024]{2,1,0:T(8,128)S(1)}, u32[]{:S(2)}, u32[]{:S(2)}) collective-permute-start(f32[1,256,1024]{2,1,0:T(8,128)S(1)} %get-tuple-element.8), channel_id=1, source_target_pairs={{4,0},{8,4},{12,8},{16,12},{20,16},{24,20},{28,24},{5,1},{9,5},{13... | collective-permute-start | bytes 3145736 | tf_op jit(solution)/shard_map/ppermute | solution.py:185
  50.9 5.0 %collective-permute-start.8 = (f32[64,1024]{1,0:T(8,128)S(1)}, f32[64,1024]{1,0:T(8,128)S(1)}, u32[]{:S(2)}, u32[]{:S(2)}) collective-permute-start(f32[64,1024]{1,0:T(8,128)S(1)} %collective-permute-done.6), channel_id=1, source_target_pairs={{0,4},{4,0},{8,12},{12,8},{16,20},{20,16},{24,28},{28,24},{1,5},{5... | collective-permute-start | bytes 786440 | tf_op jit(solution)/shard_map/ppermute | solution.py:57
  50.9 19.5 %collective-permute-start.11 = (f32[64,1024]{1,0:T(8,128)S(1)}, f32[64,1024]{1,0:T(8,128)S(1)}, u32[]{:S(2)}, u32[]{:S(2)}) collective-permute-start(f32[64,1024]{1,0:T(8,128)S(1)} %collective-permute-done.10), channel_id=1, source_target_pairs={{0,16},{4,20},{8,24},{12,28},{16,0},{20,4},{24,8},{28,12},{1,17},{... | collective-permute-start | bytes 786440 | tf_op jit(solution)/shard_map/ppermute | solution.py:53
  53.5 17.7 %collective-permute-start.9 = (f32[64,1024]{1,0:T(8,128)S(1)}, f32[64,1024]{1,0:T(8,128)S(1)}, u32[]{:S(2)}, u32[]{:S(2)}) collective-permute-start(f32[64,1024]{1,0:T(8,128)S(1)} %collective-permute-done.7), channel_id=1, source_target_pairs={{0,4},{4,0},{8,12},{12,8},{16,20},{20,16},{24,28},{28,24},{1,5},{5... | collective-permute-start | bytes 786440 | tf_op jit(solution)/shard_map/ppermute | solution.py:58
  55.9 17.5 %collective-permute-start.12 = (f32[64,1024]{1,0:T(8,128)S(1)}, f32[64,1024]{1,0:T(8,128)S(1)}, u32[]{:S(2)}, u32[]{:S(2)}) collective-permute-start(f32[64,1024]{1,0:T(8,128)S(1)} %collective-permute-done.10), channel_id=1, source_target_pairs={{0,4},{4,0},{8,12},{12,8},{16,20},{20,16},{24,28},{28,24},{1,5},{5... | collective-permute-start | bytes 786440 | tf_op jit(solution)/shard_map/ppermute | solution.py:57
  83.3 16.8 %collective-permute-start.16 = (f32[2,256,256]{2,1,0:T(8,128)S(1)}, f32[2,256,256]{2,1,0:T(8,128)S(1)}, u32[]{:S(2)}, u32[]{:S(2)}) collective-permute-start(f32[2,256,256]{2,1,0:T(8,128)S(1)} %get-tuple-element.16), channel_id=1, source_target_pairs={{0,1},{1,2},{2,3},{3,0},{4,5},{5,6},{6,7},{7,4},{8,9},{9,10},{10,1... | collective-permute-start | bytes 1572872 | tf_op jit(solution)/shard_map/ppermute | solution.py:14
  83.4 27.5 %collective-permute-start.17 = (f32[2,256,256]{2,1,0:T(8,128)S(1)}, f32[2,256,256]{2,1,0:T(8,128)S(1)}, u32[]{:S(2)}, u32[]{:S(2)}) collective-permute-start(f32[2,256,256]{2,1,0:T(8,128)S(1)} %get-tuple-element.16), channel_id=1, source_target_pairs={{0,3},{1,0},{2,1},{3,2},{4,7},{5,4},{6,5},{7,6},{8,11},{9,8},{10,9... | collective-permute-start | bytes 1572872 | tf_op jit(solution)/shard_map/ppermute | solution.py:14
  87.2 56.5 %collective-permute-start.18 = (f32[2,256,256]{2,1,0:T(8,128)S(1)}, f32[2,256,256]{2,1,0:T(8,128)S(1)}, u32[]{:S(2)}, u32[]{:S(2)}) collective-permute-start(f32[2,256,256]{2,1,0:T(8,128)S(1)} %get-tuple-element.16), channel_id=1, source_target_pairs={{0,2},{1,3},{2,0},{3,1},{4,6},{5,7},{6,4},{7,5},{8,10},{9,11},{10,... | collective-permute-start | bytes 1572872 | tf_op jit(solution)/shard_map/ppermute | solution.py:14
  93.9 85.3 %collective-permute-start.14 = (f32[2,256,256]{2,1,0:T(8,128)S(1)}, f32[2,256,256]{2,1,0:T(8,128)S(1)}, u32[]{:S(2)}, u32[]{:S(2)}) collective-permute-start(f32[2,256,256]{2,1,0:T(8,128)S(1)} %fusion.12), channel_id=1, source_target_pairs={{0,1},{1,2},{2,3},{3,0},{4,5},{5,6},{6,7},{7,4},{8,9},{9,10},{10,1... | collective-permute-start | bytes 1572872 | tf_op jit(solution)/shard_map/ppermute | solution.py:14
  94.5 85.8 %collective-permute-start.15 = (f32[2,256,256]{2,1,0:T(8,128)S(1)}, f32[2,256,256]{2,1,0:T(8,128)S(1)}, u32[]{:S(2)}, u32[]{:S(2)}) collective-permute-start(f32[2,256,256]{2,1,0:T(8,128)S(1)} %fusion.10), channel_id=1, source_target_pairs={{0,3},{1,0},{2,1},{3,2},{4,7},{5,4},{6,5},{7,6},{8,11},{9,8},{10,9... | collective-permute-start | bytes 1572872 | tf_op jit(solution)/shard_map/ppermute | solution.py:14
  100.2 76.3 %collective-permute-start.19 = (f32[2,256,256]{2,1,0:T(8,128)S(1)}, f32[2,256,256]{2,1,0:T(8,128)S(1)}, u32[]{:S(2)}, u32[]{:S(2)}) collective-permute-start(f32[2,256,256]{2,1,0:T(8,128)S(1)} %fusion.6), channel_id=1, source_target_pairs={{0,2},{1,3},{2,0},{3,1},{4,6},{5,7},{6,4},{7,5},{8,10},{9,11},{10,... | collective-permute-start | bytes 1572872 | tf_op jit(solution)/shard_map/ppermute | solution.py:14
  159.7 28.1 %collective-permute-start.23 = (f32[1,256]{1,0:T(1,128)S(1)}, f32[1,256]{1,0:T(1,128)S(1)}, u32[]{:S(2)}, u32[]{:S(2)}) collective-permute-start(f32[1,256]{1,0:T(1,128)S(1)} %get-tuple-element.13), channel_id=1, source_target_pairs={{0,4},{4,8},{8,12},{12,16},{16,20},{20,24},{24,28},{1,5},{5,9},{9,... | collective-permute-start | bytes 3080 | tf_op jit(solution)/shard_map/ppermute | solution.py:216
  161.6 26.2 %collective-permute-start.24 = (f32[1,256]{1,0:T(1,128)S(1)}, f32[1,256]{1,0:T(1,128)S(1)}, u32[]{:S(2)}, u32[]{:S(2)}) collective-permute-start(f32[1,256]{1,0:T(1,128)S(1)} %get-tuple-element.14), channel_id=1, source_target_pairs={{4,0},{8,4},{12,8},{16,12},{20,16},{24,20},{28,24},{5,1},{9,5},{13... | collective-permute-start | bytes 3080 | tf_op jit(solution)/shard_map/ppermute | solution.py:217
  (10 other events, 66.4 us)

commit v3 on v2

--- a/solution.py
+++ b/solution.py
@@ -34,21 +34,32 @@
     return whole
 
 
-def gathered_once(block):
+def quarter_start(block):
+    leaves, quarter = lax.axis_size("leaf"), block.shape[0] // 4
+    leaf = lax.axis_index("leaf")
+    return (2 * (leaf // (leaves // 2)) + lax.rem(leaf, 2)) * quarter
+
+
+def splits(block):
+    return lax.axis_size("leaf") % 4 == 0 and block.shape[0] % 32 == 0
+
+
+def quarters(block):
+    mine = lax.dynamic_slice_in_dim(block, quarter_start(block), block.shape[0] // 4, 0)
+    return [shifted(mine, "mat", step) for step in shifts_of(lax.axis_size("mat"))]
+
+
+def swapped(block, own):
     leaves, count = lax.axis_size("leaf"), lax.axis_size("mat")
     size = block.shape[0]
-    if leaves % 4 or size % 32:
-        return gathered(block, "mat", 0)
     half, quarter = leaves // 2, size // 4
     leaf, me = lax.axis_index("leaf"), lax.axis_index("mat")
     upper, core = leaf // half, lax.rem(leaf, 2)
     across = [(i, (i + half) % leaves) for i in range(leaves)]
     beside = [(i, i ^ 1) for i in range(leaves)]
-    mine = lax.dynamic_slice_in_dim(block, (2 * upper + core) * quarter, quarter, 0)
-    own = [(step, shifted(mine, "mat", step)) for step in shifts_of(count)]
     shape = (size * count,) + block.shape[1:]
     whole = lax.dynamic_update_slice_in_dim(jnp.zeros(shape, block.dtype), block, me * size, 0)
-    for step, part in own:
+    for step, part in zip(shifts_of(count), own):
         start = lax.rem(me + count - step, count) * size
         other = lax.ppermute(part, "leaf", across)
         pieces = (
@@ -168,7 +179,9 @@
     count = lax.axis_size("mat")
     forward, backward = edge_rows(parent_state)
     row_start = column * slab_rows
-    full_dyn = gathered_once(dynamics)
+    split = splits(dynamics)
+    if split:
+        own_quarters = quarters(dynamics)
     weights = prob_weight.astype(jnp.float32)
     my_parents = lax.dynamic_slice_in_dim(parent_of, leaf_index * leaf_dev, leaf_dev, 0)
     my_weights = lax.dynamic_slice_in_dim(weights, leaf_index * leaf_dev, leaf_dev, 0)
@@ -183,6 +196,16 @@
     low, own, top = leaf_sums(member, leaf_value, par_dev)
     from_low = lax.ppermute(top, "leaf", forward)
     from_high = lax.ppermute(low, "leaf", backward)
+    from_low, from_high, parent_state = lax.optimization_barrier(
+        (from_low, from_high, parent_state)
+    )
+    if split:
+        from_low, from_high, own_quarters = lax.optimization_barrier(
+            (from_low, from_high, own_quarters)
+        )
+        full_dyn = swapped(dynamics, own_quarters)
+    else:
+        full_dyn = gathered(dynamics, "mat", 0)
     pads = [jnp.zeros_like(own[:1])] * (par_dev - 1)
     beside = jnp.concatenate([from_low] + pads) + jnp.concatenate(pads + [from_high])
     expected = (own + beside) / totals[:, None, None]

time: 189 us -> 189 us (level)
  the two profiles are of different devices: /device:TPU:2 before, /device:TPU:0 now
where the time goes in v3:
time: 189 us
  waiting for transfers between devices  102 us (54%)
  starting transfers between devices  31.7 us (17%)
  matrix products  19.2 us (10%)
  Pallas kernels  19 us (10%)
  local copies, waits for them, and re-layouts  10.5 us (6%)
  other arithmetic  4.58 us (2%)
    ppermute x12, waiting for transfers between devices, shifted(): lax.ppermute(block, axis, [(i, (i + step) % count) for i in range(count)])  102 us
    ppermute x12, starting transfers between devices, shifted(): lax.ppermute(block, axis, [(i, (i + step) % count) for i in range(count)])  18.2 us
    pallas_call x1, Pallas kernels, inverses(): pl.pallas_call(inverse_kernel, in_specs=[pl.BlockSpec(memory_space=pltpu....  14 us
    unnamed x18, local copies, waits for them, and re-layouts  5.19 us
    pallas_call x1, Pallas kernels, leaf_sums(): pl.pallas_call(leaf_sum_kernel, grid=(rows // tile,), in_specs=[pl.BlockS...  5.03 us
    dot_general x1, matrix products, local(): jnp.einsum('prk,kj->prj', closed, full_dyn, precision=high)  5.03 us
    ppermute x3, starting transfers between devices, swapped(): other = lax.ppermute(part, 'leaf', across)  4.49 us
    dot_general x4, matrix products, value_block(): return jnp.einsum('prk,kj->prj', expected, columns, precision=high)  4.11 us
  transfers between devices with their start and end apart: 25, of which 8 were waited for; matrix products, arithmetic and copies ran while one was open for 7% of the time, Pallas kernels for 7%

profile of v3, /device:TPU:0, one launch (start us, length us, event | category | flops | bytes accessed | tf_op | source)
XLA Modules:
  0.0 188.8 jit_solution(16245833627884470760)
XLA Ops:
  2.2 3.4 %copy-done = f32[8,256,1024]{2,1,0:T(8,128)S(1)} copy-done((f32[8,256,1024]{2,1,0:T(8,128)S(1)}, f32[8,256,1024]{2,1,0:T(8,128)}, u32[]{:S(2)}) %copy-start) | copy-done | bytes 8388632
  5.6 5.0 %shard_map.112 = (f32[1,256,1024]{2,1,0:T(8,128)S(1)}, f32[2,256,1024]{2,1,0:T(8,128)S(1)}, f32[1,256,1024]{2,1,0:T(8,128)}) custom-call(f32[8,4]{1,0:T(8,128)S(1)} %broadcast_select_fusion.member_ref, f32[8,256,1024]{2,1,0:T(8,128)S(1)} %copy-done), custom_call_target="tpu_custom_call" | custom-call | tf_op jit(solution)/shard_map/pallas_call | solution.py:102
  10.6 3.3 %collective-permute-start = (f32[1,256,1024]{2,1,0:T(8,128)}, f32[1,256,1024]{2,1,0:T(8,128)}, u32[]{:S(2)}, u32[]{:S(2)}) collective-permute-start(f32[1,256,1024]{2,1,0:T(8,128)} %get-tuple-element.15), channel_id=1, source_target_pairs={{0,4},{4,8},{8,12},{12,16},{16,20},{20,24},{24,28},{1,5},{5,9},{9,... | collective-permute-start | bytes 3145736 | tf_op jit(solution)/shard_map/ppermute | solution.py:197
  15.2 1.7 constant_dynamic-slice_fusion.1
  16.9 2.4 %collective-permute-start.2 = (f32[64,1024]{1,0:T(8,128)}, f32[64,1024]{1,0:T(8,128)}, u32[]{:S(2)}, u32[]{:S(2)}) collective-permute-start(f32[64,1024]{1,0:T(8,128)} %constant_dynamic-slice_fusion.1), channel_id=1, source_target_pairs={{0,1},{1,2},{2,3},{3,0},{4,5},{5,6},{6,7},{7,4},{8,9},{9,10},{10,1... | collective-permute-start | bytes 786440 | tf_op jit(solution)/shard_map/ppermute | solution.py:14
  19.3 2.0 %collective-permute-start.3 = (f32[64,1024]{1,0:T(8,128)}, f32[64,1024]{1,0:T(8,128)}, u32[]{:S(2)}, u32[]{:S(2)}) collective-permute-start(f32[64,1024]{1,0:T(8,128)} %constant_dynamic-slice_fusion.1), channel_id=1, source_target_pairs={{0,3},{1,0},{2,1},{3,2},{4,7},{5,4},{6,5},{7,6},{8,11},{9,8},{10,9... | collective-permute-start | bytes 786440 | tf_op jit(solution)/shard_map/ppermute | solution.py:14
  24.3 4.0 %collective-permute-done.2 = f32[64,1024]{1,0:T(8,128)} collective-permute-done((f32[64,1024]{1,0:T(8,128)}, f32[64,1024]{1,0:T(8,128)}, u32[]{:S(2)}, u32[]{:S(2)}) %collective-permute-start.2) | collective-permute-done | bytes 262176 | tf_op jit(solution)/shard_map/ppermute | solution.py:14
  28.3 6.0 %collective-permute-done.3 = f32[64,1024]{1,0:T(8,128)} collective-permute-done((f32[64,1024]{1,0:T(8,128)}, f32[64,1024]{1,0:T(8,128)}, u32[]{:S(2)}, u32[]{:S(2)}) %collective-permute-start.3) | collective-permute-done | bytes 262176 | tf_op jit(solution)/shard_map/ppermute | solution.py:14
  34.3 11.2 %collective-permute-done.4 = f32[64,1024]{1,0:T(8,128)S(1)} collective-permute-done((f32[64,1024]{1,0:T(8,128)}, f32[64,1024]{1,0:T(8,128)S(1)}, u32[]{:S(2)}, u32[]{:S(2)}) %collective-permute-start.4) | collective-permute-done | bytes 262176 | tf_op jit(solution)/shard_map/ppermute | solution.py:14
  45.5 2.3 %collective-permute-start.5 = (f32[64,1024]{1,0:T(8,128)}, f32[64,1024]{1,0:T(8,128)S(1)}, u32[]{:S(2)}, u32[]{:S(2)}) collective-permute-start(f32[64,1024]{1,0:T(8,128)} %collective-permute-done.2), channel_id=1, source_target_pairs={{0,16},{4,20},{8,24},{12,28},{16,0},{20,4},{24,8},{28,12},{1,17},{... | collective-permute-start | bytes 786440 | tf_op jit(solution)/shard_map/ppermute | solution.py:64
  47.8 3.8 %collective-permute-start.21 = (f32[2,256]{1,0:T(2,128)S(1)}, f32[2,256]{1,0:T(2,128)S(1)}, u32[]{:S(2)}, u32[]{:S(2)}) collective-permute-start(f32[2,256]{1,0:T(2,128)S(1)} %copy-done.7), channel_id=1, source_target_pairs={{0,3},{1,0},{2,1},{3,2},{4,7},{5,4},{6,5},{7,6},{8,11},{9,8},{10,9... | collective-permute-start | bytes 6152 | tf_op jit(solution)/shard_map/ppermute | solution.py:14
  52.6 2.2 %add_divide_fusion = f32[2,256,1024]{2,1,0:T(8,128)S(1)} fusion(f32[2,256,1024]{2,1,0:T(8,128)S(1)} %get-tuple-element.14, f32[1,256,1024]{2,1,0:T(8,128)} %collective-permute-done.1, f32[1,256,1024]{2,1,0:T(8,128)} %collective-permute-done, f32[2]{0:T(128)S(1)} %fusion.40), kind=kLoop, calls=%fused_computation.4 | loop fusion | flops 1572864 | bytes 6291464 | tf_op jit(solution)/shard_map/div | solution.py:211
  57.7 3.3 %collective-permute-start.17 = (f32[2,256,256]{2,1,0:T(8,128)S(1)}, f32[2,256,256]{2,1,0:T(8,128)S(1)}, u32[]{:S(2)}, u32[]{:S(2)}) collective-permute-start(f32[2,256,256]{2,1,0:T(8,128)S(1)} %get-tuple-element.32), channel_id=1, source_target_pairs={{0,3},{1,0},{2,1},{3,2},{4,7},{5,4},{6,5},{7,6},{8,11},{9,8},{10,9... | collective-permute-start | bytes 1572872 | tf_op jit(solution)/shard_map/ppermute | solution.py:14
  62.3 2.0 %collective-permute-start.11 = (f32[64,1024]{1,0:T(8,128)S(1)}, f32[64,1024]{1,0:T(8,128)S(1)}, u32[]{:S(2)}, u32[]{:S(2)}) collective-permute-start(f32[64,1024]{1,0:T(8,128)S(1)} %collective-permute-done.4), channel_id=1, source_target_pairs={{0,16},{4,20},{8,24},{12,28},{16,0},{20,4},{24,8},{28,12},{1,17},{... | collective-permute-start | bytes 786440 | tf_op jit(solution)/shard_map/ppermute | solution.py:64
  64.4 9.4 %collective-permute-done.16 = f32[2,256,256]{2,1,0:T(8,128)S(1)} collective-permute-done((f32[2,256,256]{2,1,0:T(8,128)S(1)}, f32[2,256,256]{2,1,0:T(8,128)S(1)}, u32[]{:S(2)}, u32[]{:S(2)}) %collective-permute-start.16) | collective-permute-done | bytes 524320 | tf_op jit(solution)/shard_map/ppermute | solution.py:14
  73.8 9.5 %collective-permute-done.17 = f32[2,256,256]{2,1,0:T(8,128)S(1)} collective-permute-done((f32[2,256,256]{2,1,0:T(8,128)S(1)}, f32[2,256,256]{2,1,0:T(8,128)S(1)}, u32[]{:S(2)}, u32[]{:S(2)}) %collective-permute-start.17) | collective-permute-done | bytes 524320 | tf_op jit(solution)/shard_map/ppermute | solution.py:14
  84.1 22.4 %collective-permute-done.18 = f32[2,256,256]{2,1,0:T(8,128)S(1)} collective-permute-done((f32[2,256,256]{2,1,0:T(8,128)S(1)}, f32[2,256,256]{2,1,0:T(8,128)S(1)}, u32[]{:S(2)}, u32[]{:S(2)}) %collective-permute-start.18) | collective-permute-done | bytes 524320 | tf_op jit(solution)/shard_map/ppermute | solution.py:14
  106.5 14.0 %shard_map.113 = f32[2,256,256]{2,1,0:T(8,128)S(1)} custom-call(f32[256,256]{1,0:T(8,128)S(1)} %copy-done.2, f32[1024,256]{1,0:T(8,128)S(1)} %copy-done.1, f32[2,1024,256]{2,1,0:T(8,128)S(1)} %constant_dynamic-update-slice_fusion.4.side_ref), custom_call_target="tpu_custom_call" | custom-call | flops 20132659200 | bytes 4194304 | tf_op jit(solution)/shard_map/pallas_call | solution.py:150
  125.0 3.5 %fusion.43 = f32[2,1024]{1,0:T(2,128)S(1)} fusion(f32[2,1024]{1,0:T(2,128)S(1)} %constant_dynamic-update-slice_fusion, f32[1024,1024]{1,0:T(8,128)S(1)} %constant_dynamic-update-slice_fusion.10), kind=kOutput, calls=%fused_computation.81 | convolution fusion | flops 25165824 | bytes 4210688 | tf_op jit(solution)/shard_map/ij,pj->pi/dot_general | solution.py:232
  130.6 2.4 %collective-permute-start.23 = (f32[1,256]{1,0:T(1,128)S(1)}, f32[1,256]{1,0:T(1,128)S(1)}, u32[]{:S(2)}, u32[]{:S(2)}) collective-permute-start(f32[1,256]{1,0:T(1,128)S(1)} %get-tuple-element.29), channel_id=1, source_target_pairs={{0,4},{4,8},{8,12},{12,16},{16,20},{20,24},{24,28},{1,5},{5,9},{9,... | collective-permute-start | bytes 3080 | tf_op jit(solution)/shard_map/ppermute | solution.py:239
  134.4 3.8 %collective-permute-start.15 = (f32[2,256,256]{2,1,0:T(8,128)S(1)}, f32[2,256,256]{2,1,0:T(8,128)S(1)}, u32[]{:S(2)}, u32[]{:S(2)}) collective-permute-start(f32[2,256,256]{2,1,0:T(8,128)S(1)} %fusion.10), channel_id=1, source_target_pairs={{0,3},{1,0},{2,1},{3,2},{4,7},{5,4},{6,5},{7,6},{8,11},{9,8},{10,9... | collective-permute-start | bytes 1572872 | tf_op jit(solution)/shard_map/ppermute | solution.py:14
  142.6 7.9 %collective-permute-done.14 = f32[2,256,256]{2,1,0:T(8,128)S(1)} collective-permute-done((f32[2,256,256]{2,1,0:T(8,128)S(1)}, f32[2,256,256]{2,1,0:T(8,128)S(1)}, u32[]{:S(2)}, u32[]{:S(2)}) %collective-permute-start.14) | collective-permute-done | bytes 524320 | tf_op jit(solution)/shard_map/ppermute | solution.py:14
  150.6 32.0 %collective-permute-done.19 = f32[2,256,256]{2,1,0:T(8,128)S(1)} collective-permute-done((f32[2,256,256]{2,1,0:T(8,128)S(1)}, f32[2,256,256]{2,1,0:T(8,128)S(1)}, u32[]{:S(2)}, u32[]{:S(2)}) %collective-permute-start.19) | collective-permute-done | bytes 524320 | tf_op jit(solution)/shard_map/ppermute | solution.py:14
  183.7 5.0 %add_add_fusion = f32[2,256,1024]{2,1,0:T(8,128)} fusion(f32[2,256,1024]{2,1,0:T(8,128)S(1)} %fusion.4, f32[1024,1024]{1,0:T(8,128)S(1)} %constant_dynamic-update-slice_fusion.10, f32[2,256,1024]{1,2,0:T(8,128)S(1)} %fusion.42, f32[2,1024,256]{2,1,0:T(8,128)S(1)} %constant_dynamic-update-slice_fusion.8, f32[256,1024]{1,0:T(8,128)S(1)} %copy-done.5), kind=kOutput, calls=%fused_computation.3 | convolution fusion | flops 3222798336 | bytes 13631488 | tf_op jit(solution)/shard_map/prk,kj->prj/dot_general | solution.py:250
  (99 shorter events, 24.8 us)
Async XLA Ops:
  10.6 13.7 %collective-permute-start = (f32[1,256,1024]{2,1,0:T(8,128)}, f32[1,256,1024]{2,1,0:T(8,128)}, u32[]{:S(2)}, u32[]{:S(2)}) collective-permute-start(f32[1,256,1024]{2,1,0:T(8,128)} %get-tuple-element.15), channel_id=1, source_target_pairs={{0,4},{4,8},{8,12},{12,16},{16,20},{20,24},{24,28},{1,5},{5,9},{9,... | collective-permute-start | bytes 3145736 | tf_op jit(solution)/shard_map/ppermute | solution.py:197
  13.9 10.4 %collective-permute-start.1 = (f32[1,256,1024]{2,1,0:T(8,128)S(1)}, f32[1,256,1024]{2,1,0:T(8,128)}, u32[]{:S(2)}, u32[]{:S(2)}) collective-permute-start(f32[1,256,1024]{2,1,0:T(8,128)S(1)} %get-tuple-element.16), channel_id=1, source_target_pairs={{4,0},{8,4},{12,8},{16,12},{20,16},{24,20},{28,24},{5,1},{9,5},{13... | collective-permute-start | bytes 3145736 | tf_op jit(solution)/shard_map/ppermute | solution.py:198
  16.9 11.4 %collective-permute-start.2 = (f32[64,1024]{1,0:T(8,128)}, f32[64,1024]{1,0:T(8,128)}, u32[]{:S(2)}, u32[]{:S(2)}) collective-permute-start(f32[64,1024]{1,0:T(8,128)} %constant_dynamic-slice_fusion.1), channel_id=1, source_target_pairs={{0,1},{1,2},{2,3},{3,0},{4,5},{5,6},{6,7},{7,4},{8,9},{9,10},{10,1... | collective-permute-start | bytes 786440 | tf_op jit(solution)/shard_map/ppermute | solution.py:14
  19.3 15.0 %collective-permute-start.3 = (f32[64,1024]{1,0:T(8,128)}, f32[64,1024]{1,0:T(8,128)}, u32[]{:S(2)}, u32[]{:S(2)}) collective-permute-start(f32[64,1024]{1,0:T(8,128)} %constant_dynamic-slice_fusion.1), channel_id=1, source_target_pairs={{0,3},{1,0},{2,1},{3,2},{4,7},{5,4},{6,5},{7,6},{8,11},{9,8},{10,9... | collective-permute-start | bytes 786440 | tf_op jit(solution)/shard_map/ppermute | solution.py:14
  21.3 24.2 %collective-permute-start.4 = (f32[64,1024]{1,0:T(8,128)}, f32[64,1024]{1,0:T(8,128)S(1)}, u32[]{:S(2)}, u32[]{:S(2)}) collective-permute-start(f32[64,1024]{1,0:T(8,128)} %constant_dynamic-slice_fusion.1), channel_id=1, source_target_pairs={{0,2},{1,3},{2,0},{3,1},{4,6},{5,7},{6,4},{7,5},{8,10},{9,11},{10,... | collective-permute-start | bytes 786440 | tf_op jit(solution)/shard_map/ppermute | solution.py:14
  45.5 16.6 %collective-permute-start.5 = (f32[64,1024]{1,0:T(8,128)}, f32[64,1024]{1,0:T(8,128)S(1)}, u32[]{:S(2)}, u32[]{:S(2)}) collective-permute-start(f32[64,1024]{1,0:T(8,128)} %collective-permute-done.2), channel_id=1, source_target_pairs={{0,16},{4,20},{8,24},{12,28},{16,0},{20,4},{24,8},{28,12},{1,17},{... | collective-permute-start | bytes 786440 | tf_op jit(solution)/shard_map/ppermute | solution.py:64
  47.8 14.4 %collective-permute-start.6 = (f32[64,1024]{1,0:T(8,128)}, f32[64,1024]{1,0:T(8,128)S(1)}, u32[]{:S(2)}, u32[]{:S(2)}) collective-permute-start(f32[64,1024]{1,0:T(8,128)} %collective-permute-done.2), channel_id=1, source_target_pairs={{0,4},{4,0},{8,12},{12,8},{16,20},{20,16},{24,28},{28,24},{1,5},{5... | collective-permute-start | bytes 786440 | tf_op jit(solution)/shard_map/ppermute | solution.py:68
  47.8 9.3 %collective-permute-start.20 = (f32[2,256]{1,0:T(2,128)S(1)}, f32[2,256]{1,0:T(2,128)S(1)}, u32[]{:S(2)}, u32[]{:S(2)}) collective-permute-start(f32[2,256]{1,0:T(2,128)S(1)} %copy-done.7), channel_id=1, source_target_pairs={{0,1},{1,2},{2,3},{3,0},{4,5},{5,6},{6,7},{7,4},{8,9},{9,10},{10,1... | collective-permute-start | bytes 6152 | tf_op jit(solution)/shard_map/ppermute | solution.py:14
  47.8 9.9 %collective-permute-start.21 = (f32[2,256]{1,0:T(2,128)S(1)}, f32[2,256]{1,0:T(2,128)S(1)}, u32[]{:S(2)}, u32[]{:S(2)}) collective-permute-start(f32[2,256]{1,0:T(2,128)S(1)} %copy-done.7), channel_id=1, source_target_pairs={{0,3},{1,0},{2,1},{3,2},{4,7},{5,4},{6,5},{7,6},{8,11},{9,8},{10,9... | collective-permute-start | bytes 6152 | tf_op jit(solution)/shard_map/ppermute | solution.py:14
  51.7 9.3 %collective-permute-start.22 = (f32[2,256]{1,0:T(2,128)S(1)}, f32[2,256]{1,0:T(2,128)S(1)}, u32[]{:S(2)}, u32[]{:S(2)}) collective-permute-start(f32[2,256]{1,0:T(2,128)S(1)} %copy-done.7), channel_id=1, source_target_pairs={{0,2},{1,3},{2,0},{3,1},{4,6},{5,7},{6,4},{7,5},{8,10},{9,11},{10,... | collective-permute-start | bytes 6152 | tf_op jit(solution)/shard_map/ppermute | solution.py:14
  57.1 16.7 %collective-permute-start.16 = (f32[2,256,256]{2,1,0:T(8,128)S(1)}, f32[2,256,256]{2,1,0:T(8,128)S(1)}, u32[]{:S(2)}, u32[]{:S(2)}) collective-permute-start(f32[2,256,256]{2,1,0:T(8,128)S(1)} %get-tuple-element.32), channel_id=1, source_target_pairs={{0,1},{1,2},{2,3},{3,0},{4,5},{5,6},{6,7},{7,4},{8,9},{9,10},{10,1... | collective-permute-start | bytes 1572872 | tf_op jit(solution)/shard_map/ppermute | solution.py:14
  57.7 25.6 %collective-permute-start.17 = (f32[2,256,256]{2,1,0:T(8,128)S(1)}, f32[2,256,256]{2,1,0:T(8,128)S(1)}, u32[]{:S(2)}, u32[]{:S(2)}) collective-permute-start(f32[2,256,256]{2,1,0:T(8,128)S(1)} %get-tuple-element.32), channel_id=1, source_target_pairs={{0,3},{1,0},{2,1},{3,2},{4,7},{5,4},{6,5},{7,6},{8,11},{9,8},{10,9... | collective-permute-start | bytes 1572872 | tf_op jit(solution)/shard_map/ppermute | solution.py:14
  61.0 45.4 %collective-permute-start.18 = (f32[2,256,256]{2,1,0:T(8,128)S(1)}, f32[2,256,256]{2,1,0:T(8,128)S(1)}, u32[]{:S(2)}, u32[]{:S(2)}) collective-permute-start(f32[2,256,256]{2,1,0:T(8,128)S(1)} %get-tuple-element.32), channel_id=1, source_target_pairs={{0,2},{1,3},{2,0},{3,1},{4,6},{5,7},{6,4},{7,5},{8,10},{9,11},{10,... | collective-permute-start | bytes 1572872 | tf_op jit(solution)/shard_map/ppermute | solution.py:14
  62.1 21.3 %collective-permute-start.8 = (f32[64,1024]{1,0:T(8,128)}, f32[64,1024]{1,0:T(8,128)S(1)}, u32[]{:S(2)}, u32[]{:S(2)}) collective-permute-start(f32[64,1024]{1,0:T(8,128)} %collective-permute-done.3), channel_id=1, source_target_pairs={{0,16},{4,20},{8,24},{12,28},{16,0},{20,4},{24,8},{28,12},{1,17},{... | collective-permute-start | bytes 786440 | tf_op jit(solution)/shard_map/ppermute | solution.py:64
  62.3 21.7 %collective-permute-start.11 = (f32[64,1024]{1,0:T(8,128)S(1)}, f32[64,1024]{1,0:T(8,128)S(1)}, u32[]{:S(2)}, u32[]{:S(2)}) collective-permute-start(f32[64,1024]{1,0:T(8,128)S(1)} %collective-permute-done.4), channel_id=1, source_target_pairs={{0,16},{4,20},{8,24},{12,28},{16,0},{20,4},{24,8},{28,12},{1,17},{... | collective-permute-start | bytes 786440 | tf_op jit(solution)/shard_map/ppermute | solution.py:64
  73.8 47.8 %collective-permute-start.9 = (f32[64,1024]{1,0:T(8,128)}, f32[64,1024]{1,0:T(8,128)S(1)}, u32[]{:S(2)}, u32[]{:S(2)}) collective-permute-start(f32[64,1024]{1,0:T(8,128)} %collective-permute-done.3), channel_id=1, source_target_pairs={{0,4},{4,0},{8,12},{12,8},{16,20},{20,16},{24,28},{28,24},{1,5},{5... | collective-permute-start | bytes 786440 | tf_op jit(solution)/shard_map/ppermute | solution.py:68
  83.4 38.4 %collective-permute-start.12 = (f32[64,1024]{1,0:T(8,128)S(1)}, f32[64,1024]{1,0:T(8,128)S(1)}, u32[]{:S(2)}, u32[]{:S(2)}) collective-permute-start(f32[64,1024]{1,0:T(8,128)S(1)} %collective-permute-done.4), channel_id=1, source_target_pairs={{0,4},{4,0},{8,12},{12,8},{16,20},{20,16},{24,28},{28,24},{1,5},{5... | collective-permute-start | bytes 786440 | tf_op jit(solution)/shard_map/ppermute | solution.py:68
  83.4 37.1 %collective-permute-start.7 = (f32[64,1024]{1,0:T(8,128)S(1)}, f32[64,1024]{1,0:T(8,128)S(1)}, u32[]{:S(2)}, u32[]{:S(2)}) collective-permute-start(f32[64,1024]{1,0:T(8,128)S(1)} %collective-permute-done.5), channel_id=1, source_target_pairs={{0,4},{4,0},{8,12},{12,8},{16,20},{20,16},{24,28},{28,24},{1,5},{5... | collective-permute-start | bytes 786440 | tf_op jit(solution)/shard_map/ppermute | solution.py:69
  84.0 37.6 %collective-permute-start.10 = (f32[64,1024]{1,0:T(8,128)S(1)}, f32[64,1024]{1,0:T(8,128)S(1)}, u32[]{:S(2)}, u32[]{:S(2)}) collective-permute-start(f32[64,1024]{1,0:T(8,128)S(1)} %collective-permute-done.8), channel_id=1, source_target_pairs={{0,4},{4,0},{8,12},{12,8},{16,20},{20,16},{24,28},{28,24},{1,5},{5... | collective-permute-start | bytes 786440 | tf_op jit(solution)/shard_map/ppermute | solution.py:69
  106.4 15.3 %collective-permute-start.13 = (f32[64,1024]{1,0:T(8,128)S(1)}, f32[64,1024]{1,0:T(8,128)S(1)}, u32[]{:S(2)}, u32[]{:S(2)}) collective-permute-start(f32[64,1024]{1,0:T(8,128)S(1)} %collective-permute-done.11), channel_id=1, source_target_pairs={{0,4},{4,0},{8,12},{12,8},{16,20},{20,16},{24,28},{28,24},{1,5},{5... | collective-permute-start | bytes 786440 | tf_op jit(solution)/shard_map/ppermute | solution.py:69
  130.6 11.3 %collective-permute-start.23 = (f32[1,256]{1,0:T(1,128)S(1)}, f32[1,256]{1,0:T(1,128)S(1)}, u32[]{:S(2)}, u32[]{:S(2)}) collective-permute-start(f32[1,256]{1,0:T(1,128)S(1)} %get-tuple-element.29), channel_id=1, source_target_pairs={{0,4},{4,8},{8,12},{12,16},{16,20},{20,24},{24,28},{1,5},{5,9},{9,... | collective-permute-start | bytes 3080 | tf_op jit(solution)/shard_map/ppermute | solution.py:239
  134.3 16.2 %collective-permute-start.14 = (f32[2,256,256]{2,1,0:T(8,128)S(1)}, f32[2,256,256]{2,1,0:T(8,128)S(1)}, u32[]{:S(2)}, u32[]{:S(2)}) collective-permute-start(f32[2,256,256]{2,1,0:T(8,128)S(1)} %fusion.12), channel_id=1, source_target_pairs={{0,1},{1,2},{2,3},{3,0},{4,5},{5,6},{6,7},{7,4},{8,9},{9,10},{10,1... | collective-permute-start | bytes 1572872 | tf_op jit(solution)/shard_map/ppermute | solution.py:14
  134.4 49.3 %collective-permute-start.15 = (f32[2,256,256]{2,1,0:T(8,128)S(1)}, f32[2,256,256]{2,1,0:T(8,128)S(1)}, u32[]{:S(2)}, u32[]{:S(2)}) collective-permute-start(f32[2,256,256]{2,1,0:T(8,128)S(1)} %fusion.10), channel_id=1, source_target_pairs={{0,3},{1,0},{2,1},{3,2},{4,7},{5,4},{6,5},{7,6},{8,11},{9,8},{10,9... | collective-permute-start | bytes 1572872 | tf_op jit(solution)/shard_map/ppermute | solution.py:14
  140.6 41.9 %collective-permute-start.19 = (f32[2,256,256]{2,1,0:T(8,128)S(1)}, f32[2,256,256]{2,1,0:T(8,128)S(1)}, u32[]{:S(2)}, u32[]{:S(2)}) collective-permute-start(f32[2,256,256]{2,1,0:T(8,128)S(1)} %fusion.6), channel_id=1, source_target_pairs={{0,2},{1,3},{2,0},{3,1},{4,6},{5,7},{6,4},{7,5},{8,10},{9,11},{10,... | collective-permute-start | bytes 1572872 | tf_op jit(solution)/shard_map/ppermute | solution.py:14
  (10 other events, 135.2 us)
